TPU v7x, 32 devices: a whole 2x2x4 slice. The times are simulated.
32 devices in a mesh: dp: 16 (over z, y, x), mp: 2 (over core).
Axes of the slice: x: 2, y: 2, z: 4, core: 2. Of those that a mesh axis runs over, the one named last changes fastest.
Arguments:
- tokens: bfloat16 [4096, 768], P(('dp', 'mp')), may hold values from -6 to 6
- cotangent: bfloat16 [4096, 768], P(('dp', 'mp')), may hold values from -6 to 6
- char_ids: int32 [4096, 20], P(('dp', 'mp')), may hold values from 0 to 511
- char_lens: int32 [4096], P(('dp', 'mp')), may hold values from 1 to 20, as said below
- w_qkv: bfloat16 [1, 768, 3, 768], P(None, None, None, 'mp'), may hold values from -0.21875 to 0.21875
- b_qkv: bfloat16 [1, 2, 768], P(None, None, 'mp'), may hold values from -3 to 3
- w_out: bfloat16 [1, 768, 768], P(None, 'mp'), may hold values from -0.875 to 0.875
- w_up: bfloat16 [1, 768, 3072], P(None, None, 'mp'), may hold values from -0.21875 to 0.21875
- up_bias: bfloat16 [1, 3072], P(None, 'mp'), may hold values from -3 to 3
- w_down: bfloat16 [1, 3072, 768], P(None, 'mp'), may hold values from -0.109375 to 0.109375
- res_bias: bfloat16 [1, 3, 768], replicated, may hold values from -3 to 3
- norm_gain: bfloat16 [1, 3, 768], replicated, may hold values from 0.5 to 1.5
- norm_bias: bfloat16 [1, 3, 768], replicated, may hold values from -1.75 to 1.75
- char_table: bfloat16 [512, 256], replicated, may hold values from -6 to 6
- gru_in: bfloat16 [1, 2, 256, 1152], replicated, may hold values from -0.375 to 0.375
- gru_hid: bfloat16 [1, 2, 384, 1152], replicated, may hold values from -0.3125 to 0.3125
- gru_bias: bfloat16 [1, 2, 2, 1152], replicated, may hold values from -3 to 3
- conv_w: bfloat16 [1, 3, 1536, 768], replicated, may hold values from -0.09375 to 0.09375
Outputs:
- out: bfloat16 [4096, 768], P(('dp', 'mp'))
- tokens_grad: float32 [4096, 768], P(('dp', 'mp'))
- w_qkv_grad: float32 [1, 768, 3, 768], P(None, 'dp', None, 'mp')
- b_qkv_grad: float32 [1, 2, 768], P(None, None, 'mp')
- w_out_grad: float32 [1, 768, 768], P(None, 'mp', 'dp')
- w_up_grad: float32 [1, 768, 3072], P(None, 'dp', 'mp')
- up_bias_grad: float32 [1, 3072], P(None, 'mp')
- w_down_grad: float32 [1, 3072, 768], P(None, 'mp', 'dp')
- res_bias_grad: float32 [1, 3, 768], replicated
- norm_gain_grad: float32 [1, 3, 768], replicated
- norm_bias_grad: float32 [1, 3, 768], replicated
- char_table_grad: float32 [512, 256], replicated
- gru_in_grad: float32 [1, 2, 256, 1152], replicated
- gru_hid_grad: float32 [1, 2, 384, 1152], replicated
- gru_bias_grad: float32 [1, 2, 2, 1152], replicated
- conv_w_grad: float32 [1, 3, 1536, 768], P(None, None, 'dp')
Inputs may be any that keep to these rules, and one draw needn't show every extreme that they name: `char_lens`: every block of 128 consecutive tokens holds a token of 20 characters.
All inputs are finite; a program needn't handle non-finite values.
Results may differ from a plain program's by a relative error of at most 0.018.
Values may be sent and summed in bfloat16 or wider, within the bound.
No kernel may reach another device: no remote copies, remote signals or barrier semaphores. Data moves between devices by JAX's collectives and lax.ppermute only.
A program may use at most 256 MiB of HBM per device.

v0:
```python
import jax
import jax.numpy as jnp
from jax import lax
from jax.sharding import PartitionSpec as P

HD = 64


PRECISE = lax.Precision.HIGHEST
EPSILON = 1e-05


def padded_2(cells, sides, width):
    for axis, dim in sides:
        count = lax.axis_size(axis)
        ends = count - 1
        head = lax.slice_in_dim(cells, 0, width, axis=dim)
        tail = lax.slice_in_dim(cells, cells.shape[dim] - width, cells.shape[dim], axis=dim)
        cells = jnp.concatenate(
            [
                lax.ppermute(tail, axis, [(i, (i + 1) % count) for i in range(ends)]),
                cells,
                lax.ppermute(head, axis, [((i + 1) % count, i) for i in range(ends)]),
            ],
            axis=dim,
        )
    return cells


def norm_apply(totals, scales, offsets):
    centre = jnp.mean(totals, -1, keepdims=True)
    centred = totals - centre
    spread = jnp.mean(centred * centred, -1, keepdims=True)
    return centred * lax.rsqrt(spread + EPSILON) * scales + offsets


def gelu_apply(inputs):
    return jax.nn.gelu(inputs, approximate=True)


def gate_apply(drive_step, recur_step, carried, mask_step):
    width = carried.shape[-1]
    reset = jax.nn.sigmoid(drive_step[:, :width] + recur_step[:, :width])
    update = jax.nn.sigmoid(drive_step[:, width : 2 * width] + recur_step[:, width : 2 * width])
    fresh = jnp.tanh(drive_step[:, 2 * width :] + reset * recur_step[:, 2 * width :])
    moved = (1.0 - update) * fresh + update * carried
    return mask_step * moved + (1.0 - mask_step) * carried


def gather_rows(values):
    return lax.all_gather(values, "mp", axis=0, tiled=True)


def spread_rows(values):
    return lax.psum_scatter(
        values.astype(jnp.bfloat16), "mp", scatter_dimension=0, tiled=True
    ).astype(jnp.float32)


def token_rims(values):
    return padded_2(values, (("mp", 0),), 1)


def gru_run(embedded, in_weight, hid_weight, gru_shift, char_mask, direction):
    slot_count = char_mask.shape[0]
    row_count = char_mask.shape[1]
    drive_all = (
        jnp.dot(embedded, in_weight[direction], preferred_element_type=jnp.float32)
        + gru_shift[direction, 0]
    )
    drive_all = drive_all.reshape(slot_count, row_count, drive_all.shape[-1])
    hid_matrix = hid_weight[direction]
    hid_offset = gru_shift[direction, 1]

    def advance(carried, inputs):
        drive_step, mask_step = inputs
        recur_step = (
            jnp.dot(carried.astype(jnp.bfloat16), hid_matrix, preferred_element_type=jnp.float32)
            + hid_offset
        )
        return (gate_apply(drive_step, recur_step, carried, mask_step), carried)

    initial = jnp.zeros((row_count, hid_matrix.shape[0]), jnp.float32)
    last_state, previous = lax.scan(
        advance, initial, (drive_all, char_mask), reverse=direction == 1
    )
    return (last_state, drive_all, previous)


def gru_back(embedded, in_weight, hid_weight, gru_shift, char_mask, direction, end_grad):
    _, drive_all, previous = gru_run(
        embedded, in_weight, hid_weight, gru_shift, char_mask, direction
    )
    hid_matrix = hid_weight[direction]
    hid_offset = gru_shift[direction, 1]

    def retreat(carry_in, inputs):
        state_grad, matrix_grad, offset_grad = carry_in
        drive_step, mask_step, prior = inputs
        prior_low = prior.astype(jnp.bfloat16)
        recur_step = jnp.dot(prior_low, hid_matrix, preferred_element_type=jnp.float32) + hid_offset
        _, pullback = jax.vjp(gate_apply, drive_step, recur_step, prior, mask_step)
        drive_grad, recur_grad, prior_grad, _ = pullback(state_grad)
        recur_low = recur_grad.astype(jnp.bfloat16)
        prior_grad = prior_grad + jnp.dot(
            recur_low, hid_matrix.T, preferred_element_type=jnp.float32
        )
        matrix_grad = matrix_grad + jnp.dot(
            prior_low.T, recur_low, preferred_element_type=jnp.float32
        )
        offset_grad = offset_grad + jnp.sum(recur_low.astype(jnp.float32), 0)
        return ((prior_grad, matrix_grad, offset_grad), drive_grad)

    initial = (
        end_grad,
        jnp.zeros(hid_matrix.shape, jnp.float32),
        jnp.zeros((hid_matrix.shape[1],), jnp.float32),
    )
    (_, matrix_grad, offset_grad), drive_grads = lax.scan(
        retreat, initial, (drive_all, char_mask, previous), reverse=direction == 0
    )
    drive_low = drive_grads.reshape(-1, drive_grads.shape[-1]).astype(jnp.bfloat16)
    input_grad = jnp.dot(embedded.T, drive_low, preferred_element_type=jnp.float32)
    embed_grad = jnp.dot(drive_low, in_weight[direction].T, preferred_element_type=jnp.float32)
    drive_offset = jnp.sum(drive_low.astype(jnp.float32), 0)
    return (input_grad, matrix_grad, jnp.stack([drive_offset, offset_grad]), embed_grad)


def project_heads(gathered, qkv_weight, qkv_shift):
    seq_len = gathered.shape[0]
    projected = jnp.einsum("sd,dkn->skn", gathered, qkv_weight, preferred_element_type=jnp.float32)
    head_shape = (seq_len, qkv_weight.shape[2] // HD, HD)
    queries = (projected[:, 0] + qkv_shift[0]).astype(jnp.bfloat16).reshape(head_shape)
    keys_low = projected[:, 1].astype(jnp.bfloat16).reshape(head_shape)
    values_low = (projected[:, 2] + qkv_shift[1]).astype(jnp.bfloat16).reshape(head_shape)
    return (queries, keys_low, values_low)


def score_heads(queries, keys_low):
    return jnp.einsum(
        "qhd,khd->hqk", queries, keys_low, preferred_element_type=jnp.float32
    ) * HD ** (-0.5)


def mix_heads(probs_low, values_low):
    mixed = jnp.einsum("hqk,khd->qhd", probs_low, values_low, preferred_element_type=jnp.float32)
    return mixed.reshape(mixed.shape[0], -1).astype(jnp.bfloat16)


def conv_apply(padded, conv_kernel, count):
    total = jnp.dot(padded[0:count], conv_kernel[0], preferred_element_type=jnp.float32)
    total = total + jnp.dot(
        padded[1 : count + 1], conv_kernel[1], preferred_element_type=jnp.float32
    )
    return total + jnp.dot(
        padded[2 : count + 2], conv_kernel[2], preferred_element_type=jnp.float32
    )


def layer_forward(layer_in, weights, embedded, char_mask):
    (
        qkv_weight,
        qkv_shift,
        out_weight,
        up_weight,
        up_shift,
        down_weight,
        res_shift,
        gains,
        offsets,
        in_weight,
        hid_weight,
        gru_shift,
        conv_kernel,
    ) = weights
    local_rows = layer_in.shape[0]
    gathered = gather_rows(layer_in.astype(jnp.bfloat16))
    queries, keys_low, values_low = project_heads(gathered, qkv_weight, qkv_shift)
    scores = score_heads(queries, keys_low)
    peak = jnp.max(scores, -1, keepdims=True)
    log_total = peak + jnp.log(jnp.sum(jnp.exp(scores - peak), -1, keepdims=True))
    probs_low = jnp.exp(scores - log_total).astype(jnp.bfloat16)
    mixed_low = mix_heads(probs_low, values_low)
    attn_out = spread_rows(jnp.dot(mixed_low, out_weight, preferred_element_type=jnp.float32))
    first_sum = layer_in + attn_out + res_shift[0]
    first_norm = norm_apply(first_sum, gains[0], offsets[0])
    norm_rows = gather_rows(first_norm.astype(jnp.bfloat16))
    pre_act = jnp.dot(norm_rows, up_weight, preferred_element_type=jnp.float32) + up_shift
    ffn_out = spread_rows(
        jnp.dot(
            gelu_apply(pre_act).astype(jnp.bfloat16),
            down_weight,
            preferred_element_type=jnp.float32,
        )
    )
    second_sum = first_norm + ffn_out + res_shift[1]
    second_norm = norm_apply(second_sum, gains[1], offsets[1])
    forward_last = gru_run(embedded, in_weight, hid_weight, gru_shift, char_mask, 0)[0]
    backward_last = gru_run(embedded, in_weight, hid_weight, gru_shift, char_mask, 1)[0]
    joined = jnp.concatenate([second_norm, forward_last, backward_last], 1).astype(jnp.bfloat16)
    padded = token_rims(joined)
    conv_raw = conv_apply(padded, conv_kernel, local_rows) + res_shift[2]
    third_sum = second_norm + gelu_apply(conv_raw)
    result = norm_apply(third_sum, gains[2], offsets[2])
    saved = (
        gathered,
        queries,
        keys_low,
        values_low,
        log_total,
        first_sum,
        norm_rows,
        pre_act,
        second_sum,
        padded,
        conv_raw,
        third_sum,
    )
    return (result, saved)


def layer_backward(upstream, saved, weights, embedded, char_mask):
    (
        qkv_weight,
        qkv_shift,
        out_weight,
        up_weight,
        up_shift,
        down_weight,
        res_shift,
        gains,
        offsets,
        in_weight,
        hid_weight,
        gru_shift,
        conv_kernel,
    ) = weights
    (
        gathered,
        queries,
        keys_low,
        values_low,
        log_total,
        first_sum,
        norm_rows,
        pre_act,
        second_sum,
        padded,
        conv_raw,
        third_sum,
    ) = saved
    local_rows = upstream.shape[0]
    model_width = upstream.shape[1]
    _, norm_pull = jax.vjp(norm_apply, third_sum, gains[2], offsets[2])
    third_grad, gain_two, offset_two = norm_pull(upstream)
    conv_grad = jax.vjp(gelu_apply, conv_raw)[1](third_grad)[0]
    conv_low = conv_grad.astype(jnp.bfloat16)
    shift_two = jnp.sum(conv_low.astype(jnp.float32), 0)
    kernel_grad = jnp.stack(
        [
            jnp.dot(padded[k : k + local_rows].T, conv_low, preferred_element_type=jnp.float32)
            for k in range(3)
        ]
    )
    conv_padded = token_rims(conv_low)
    joined_grad = jnp.dot(
        conv_padded[2 : local_rows + 2], conv_kernel[0].T, preferred_element_type=jnp.float32
    )
    joined_grad = joined_grad + jnp.dot(
        conv_padded[1 : local_rows + 1], conv_kernel[1].T, preferred_element_type=jnp.float32
    )
    joined_grad = joined_grad + jnp.dot(
        conv_padded[0:local_rows], conv_kernel[2].T, preferred_element_type=jnp.float32
    )
    second_grad = third_grad + joined_grad[:, :model_width]
    char_grad = joined_grad[:, model_width:]
    gru_width = char_grad.shape[1] // 2
    in_grads, hid_grads, shift_grads = ([], [], [])
    embed_grad = jnp.zeros((embedded.shape[0], embedded.shape[1]), jnp.float32)
    for direction in range(2):
        end_grad = char_grad[:, direction * gru_width : (direction + 1) * gru_width]
        input_grad, matrix_grad, offset_pair, embed_part = gru_back(
            embedded, in_weight, hid_weight, gru_shift, char_mask, direction, end_grad
        )
        in_grads.append(input_grad)
        hid_grads.append(matrix_grad)
        shift_grads.append(offset_pair)
        embed_grad = embed_grad + embed_part
    _, norm_pull = jax.vjp(norm_apply, second_sum, gains[1], offsets[1])
    second_res, gain_one, offset_one = norm_pull(second_grad)
    shift_one = jnp.sum(second_res, 0)
    ffn_rows = gather_rows(second_res.astype(jnp.bfloat16))
    activ_low = gelu_apply(pre_act).astype(jnp.bfloat16)
    down_grad = jnp.dot(activ_low.T, ffn_rows, preferred_element_type=jnp.float32)
    activ_grad = jnp.dot(ffn_rows, down_weight.T, preferred_element_type=jnp.float32)
    pre_grad = jax.vjp(gelu_apply, pre_act)[1](activ_grad)[0]
    pre_low = pre_grad.astype(jnp.bfloat16)
    up_shift_grad = jnp.sum(pre_low.astype(jnp.float32), 0)
    up_grad = jnp.dot(norm_rows.T, pre_low, preferred_element_type=jnp.float32)
    first_grad = second_res + spread_rows(
        jnp.dot(pre_low, up_weight.T, preferred_element_type=jnp.float32)
    )
    _, norm_pull = jax.vjp(norm_apply, first_sum, gains[0], offsets[0])
    first_res, gain_zero, offset_zero = norm_pull(first_grad)
    shift_zero = jnp.sum(first_res, 0)
    attn_rows = gather_rows(first_res.astype(jnp.bfloat16))
    probs = jnp.exp(score_heads(queries, keys_low) - log_total)
    probs_low = probs.astype(jnp.bfloat16)
    mixed_low = mix_heads(probs_low, values_low)
    out_grad = jnp.dot(mixed_low.T, attn_rows, preferred_element_type=jnp.float32)
    mixed_grad = (
        jnp.dot(attn_rows, out_weight.T, preferred_element_type=jnp.float32)
        .astype(jnp.bfloat16)
        .reshape(queries.shape)
    )
    probs_grad = jnp.einsum(
        "qhd,khd->hqk", mixed_grad, values_low, preferred_element_type=jnp.float32
    )
    values_grad = jnp.einsum(
        "hqk,qhd->khd", probs_low, mixed_grad, preferred_element_type=jnp.float32
    )
    score_grad = probs * (probs_grad - jnp.sum(probs * probs_grad, -1, keepdims=True))
    score_low = score_grad.astype(jnp.bfloat16)
    query_grad = jnp.einsum(
        "hqk,khd->qhd", score_low, keys_low, preferred_element_type=jnp.float32
    ) * HD ** (-0.5)
    key_grad = jnp.einsum(
        "hqk,qhd->khd", score_low, queries, preferred_element_type=jnp.float32
    ) * HD ** (-0.5)
    seq_len = queries.shape[0]
    proj_grad = (
        jnp.stack([query_grad, key_grad, values_grad], 1)
        .reshape(seq_len, 3, -1)
        .astype(jnp.bfloat16)
    )
    proj_sums = jnp.sum(proj_grad.astype(jnp.float32), 0)
    qkv_shift_grad = jnp.stack([proj_sums[0], proj_sums[2]])
    qkv_grad = jnp.einsum("sd,skn->dkn", gathered, proj_grad, preferred_element_type=jnp.float32)
    input_rows = jnp.einsum(
        "skn,dkn->sd", proj_grad, qkv_weight, preferred_element_type=jnp.float32
    )
    layer_grad = first_res + spread_rows(input_rows)
    grads = (
        qkv_grad,
        qkv_shift_grad,
        out_grad,
        up_grad,
        up_shift_grad,
        down_grad,
        jnp.stack([shift_zero, shift_one, shift_two]),
        jnp.stack([gain_zero, gain_one, gain_two]),
        jnp.stack([offset_zero, offset_one, offset_two]),
        jnp.stack(in_grads),
        jnp.stack(hid_grads),
        jnp.stack(shift_grads),
        kernel_grad,
    )
    return (layer_grad, grads, embed_grad)


def per_device(
    tokens,
    cotangent,
    char_ids,
    char_lens,
    w_qkv,
    b_qkv,
    w_out,
    w_up,
    up_bias,
    w_down,
    res_bias,
    norm_gain,
    norm_bias,
    char_table,
    gru_in,
    gru_hid,
    gru_bias,
    conv_w,
):
    char_count = char_ids.shape[1]
    vocab_size = char_table.shape[0]
    ids_major = char_ids.T.reshape(-1)
    one_hot = ids_major[:, None] == jnp.arange(vocab_size, dtype=jnp.int32)[None, :]
    embedded = jnp.dot(
        one_hot.astype(jnp.bfloat16), char_table, preferred_element_type=jnp.float32
    ).astype(jnp.bfloat16)
    char_mask = (jnp.arange(char_count, dtype=jnp.int32)[:, None] < char_lens[None, :]).astype(
        jnp.float32
    )[:, :, None]
    stacked = (
        w_qkv,
        b_qkv.astype(jnp.float32),
        w_out,
        w_up,
        up_bias.astype(jnp.float32),
        w_down,
        res_bias.astype(jnp.float32),
        norm_gain.astype(jnp.float32),
        norm_bias.astype(jnp.float32),
        gru_in,
        gru_hid,
        gru_bias.astype(jnp.float32),
        conv_w,
    )
    layer_count = w_qkv.shape[0]
    current = tokens.astype(jnp.float32)
    layer = 0
    weights = tuple((member[layer] for member in stacked))
    current, saved = layer_forward(current, weights, embedded, char_mask)
    saved_all = [saved]
    result = current.astype(jnp.bfloat16)
    upstream = cotangent.astype(jnp.float32)
    grads_by_layer = [None] * layer_count
    embed_total = jnp.zeros((embedded.shape[0], embedded.shape[1]), jnp.float32)
    for layer in reversed(range(layer_count)):
        weights = tuple((member[layer] for member in stacked))
        upstream, grads, embed_grad = layer_backward(
            upstream, saved_all[layer], weights, embedded, char_mask
        )
        grads_by_layer[layer] = grads
        embed_total = embed_grad
    merged = [jnp.stack([grads_by_layer[0][index]]) for index in range(13)]
    table_grad = jnp.dot(one_hot.astype(jnp.float32).T, embed_total, precision=PRECISE)
    qkv_out, out_out, up_out, down_out = (
        lax.psum_scatter(merged[0], "dp", scatter_dimension=1, tiled=True),
        lax.psum_scatter(merged[2], "dp", scatter_dimension=2, tiled=True),
        lax.psum_scatter(merged[3], "dp", scatter_dimension=1, tiled=True),
        lax.psum_scatter(merged[5], "dp", scatter_dimension=2, tiled=True),
    )
    qkv_shift_out, up_shift_out = lax.psum((merged[1], merged[4]), "dp")
    res_out, gain_out, offset_out, table_out, in_out, hid_out, gru_shift_out = lax.psum(
        (merged[6], merged[7], merged[8], table_grad, merged[9], merged[10], merged[11]),
        ("dp", "mp"),
    )
    kernel_part = lax.psum_scatter(merged[12], ("dp", "mp"), scatter_dimension=2, tiled=True)
    kernel_out = lax.all_gather(kernel_part.astype(jnp.bfloat16), "mp", axis=2, tiled=True).astype(
        kernel_part.dtype
    )
    return (
        result,
        upstream,
        qkv_out,
        qkv_shift_out,
        out_out,
        up_out,
        up_shift_out,
        down_out,
        res_out,
        gain_out,
        offset_out,
        table_out,
        in_out,
        hid_out,
        gru_shift_out,
        kernel_out,
    )


def solution(mesh):
    return jax.shard_map(
        per_device,
        mesh=mesh,
        in_specs=(
            P(("dp", "mp"), None),
            P(("dp", "mp"), None),
            P(("dp", "mp"), None),
            P(("dp", "mp")),
            P(None, None, None, "mp"),
            P(None, None, "mp"),
            P(None, "mp", None),
            P(None, None, "mp"),
            P(None, "mp"),
            P(None, "mp", None),
            P(),
            P(),
            P(),
            P(),
            P(),
            P(),
            P(),
            P(),
        ),
        out_specs=(
            P(("dp", "mp"), None),
            P(("dp", "mp"), None),
            P(None, "dp", None, "mp"),
            P(None, None, "mp"),
            P(None, "mp", "dp"),
            P(None, "dp", "mp"),
            P(None, "mp"),
            P(None, "mp", "dp"),
            P(),
            P(),
            P(),
            P(),
            P(),
            P(),
            P(),
            P(None, None, "dp", None),
        ),
        check_vma=False,
    )
```

profile of v0, /device:TPU:0, one launch (start us, length us, event | category | flops | bytes accessed | tf_op | source)
XLA Modules:
  0.0 1246.7 jit_solution(3725856353586950248)
XLA Ops:
  25.9 6.2 convolution_add_fusion.10
  32.1 117.9 %while.95 = (s32[]{:T(128)}, f32[128,384]{1,0:T(8,128)}, f32[20,128,1]{1,2,0:T(1,128)}, f32[20,128,1152]{2,1,0:T(8,128)}, bf16[384,1152]{1,0:T(8,128)(2,1)S(1)},...) while((s32[]{:T(128)}, f32[128,384]{1,0:T(8,128)}, ...), condition=%wide.region_11.12_spmd.clone, body=%wide.region_10.11_spmd.clone.sunk | while | flops 114327680 | bytes 4440208 | solution.py:84
  150.7 7.7 convolution_add_fusion.11
  170.3 70.0 %while.94 = (s32[]{:T(128)}, f32[128,384]{1,0:T(8,128)S(1)}, f32[20,128,1]{1,2,0:T(1,128)}, f32[20,128,1152]{2,1,0:T(8,128)}, bf16[384,1152]{1,0:T(8,128)(2,1)},...) while((s32[]{:T(128)}, f32[128,384]{1,0:T(8,128)S(1)}, ...), condition=%wide.region_9.10_spmd.clone, body=%wide.region_8.9_spmd.clone.sunk | while | flops 114327680 | bytes 4440188 | solution.py:84
  248.0 3.5 collective-permute-start
  274.4 10.4 reduce-scatter.11.cloned.1.call-done
  305.2 60.5 %while.98 = (s32[]{:T(128)}, f32[128,384]{1,0:T(8,128)S(1)}, f32[20,128,384]{2,1,0:T(8,128)}, f32[20,128,1]{1,2,0:T(1,128)}, f32[20,128,1152]{2,1,0:T(8,128)}, /...) while((s32[]{:T(128)}, f32[128,384]{1,0:T(8,128)S(1)}, ...), condition=%wide.region_49.50_spmd.clone, body=%wide.region_48.49_spmd.clone.sunk | while | flops 114376832 | bytes 4833437 | solution.py:84
  365.8 4.8 convolution_bitcast_fusion.3
  370.6 12.3 copy.80
  385.4 11.9 copy.78
  402.7 61.0 %while.96 = (s32[]{:T(128)}, f32[128,384]{1,0:T(8,128)S(1)}, f32[20,128,384]{2,1,0:T(8,128)}, f32[20,128,1]{1,2,0:T(1,128)}, f32[20,128,1152]{2,1,0:T(8,128)}, /...) while((s32[]{:T(128)}, f32[128,384]{1,0:T(8,128)S(1)}, ...), condition=%wide.region_44.45_spmd.clone, body=%wide.region_43.44_spmd.clone.sunk | while | flops 114376832 | bytes 4833417 | solution.py:84
  463.8 3.9 convolution_bitcast_fusion.1
  473.7 11.2 maximum_bitcast_fusion
  486.8 3.3 broadcast.313.clone.1
  490.1 235.5 %while.97 = (s32[]{:T(128)}, f32[128,384]{1,0:T(8,128)}, f32[384,1152]{1,0:T(8,128)}, f32[1152]{0:T(1024)S(1)}, bf16[20,128,1152]{2,1,0:T(8,128)(2,1)}, /*index=...) while((s32[]{:T(128)}, f32[128,384]{1,0:T(8,128)}, ...), condition=%wide.region_47.48_spmd.clone, body=%wide.region_45.47_spmd.clone.sunk | while | flops 344016128 | bytes 17435924 | solution.py:119
  508.8 3.4 convolution_add_fusion.30
  520.6 3.4 convolution_add_fusion.30
  532.3 3.4 convolution_add_fusion.30
  544.0 3.4 convolution_add_fusion.30
  555.7 3.4 convolution_add_fusion.30
  567.4 3.5 convolution_add_fusion.30
  579.2 3.4 convolution_add_fusion.30
  590.9 3.4 convolution_add_fusion.30
  602.8 3.8 convolution_add_fusion.30
  614.9 3.4 convolution_add_fusion.30
  626.6 3.4 convolution_add_fusion.30
  638.4 3.7 convolution_add_fusion.30
  650.4 3.4 convolution_add_fusion.30
  662.1 3.4 convolution_add_fusion.30
  673.8 3.4 convolution_add_fusion.30
  685.5 3.4 convolution_add_fusion.30
  697.3 3.5 convolution_add_fusion.30
  709.3 3.5 convolution_add_fusion.30
  721.3 3.5 convolution_add_fusion.30
  725.5 3.4 broadcast.313.clone
  728.9 176.8 %while.99 = (s32[]{:T(128)}, f32[128,384]{1,0:T(8,128)S(1)}, f32[384,1152]{1,0:T(8,128)}, f32[1152]{0:T(1024)S(1)}, bf16[20,128,1152]{2,1,0:T(8,128)(2,1)}, /*in...) while((s32[]{:T(128)}, f32[128,384]{1,0:T(8,128)S(1)}, ...), condition=%wide.region_52.53_spmd.clone, body=%wide.region_50.52_spmd.clone.sunk | while | flops 344016128 | bytes 14683308 | solution.py:119
  742.0 3.2 convolution_add_fusion.34
  750.8 3.2 convolution_add_fusion.34
  759.6 3.2 convolution_add_fusion.34
  768.5 3.3 convolution_add_fusion.34
  777.3 3.3 convolution_add_fusion.34
  786.3 3.2 convolution_add_fusion.34
  795.1 3.3 convolution_add_fusion.34
  804.0 3.6 convolution_add_fusion.34
  813.2 3.2 convolution_add_fusion.34
  822.1 3.3 convolution_add_fusion.34
  831.0 3.3 convolution_add_fusion.34
  839.9 3.2 convolution_add_fusion.34
  848.7 3.2 convolution_add_fusion.34
  857.6 3.2 convolution_add_fusion.34
  866.4 3.2 convolution_add_fusion.34
  875.2 3.2 convolution_add_fusion.34
  884.0 3.2 convolution_add_fusion.34
  892.8 3.2 convolution_add_fusion.34
  901.6 3.2 convolution_add_fusion.34
  905.8 4.9 fusion.177
  912.7 5.5 fusion.108
  933.2 4.2 convert_reduce_fusion.2
  937.5 3.8 convert_reduce_fusion.3
  941.7 45.3 %all-reduce.13 = (f32[1,2,384]{2,1,0:T(2,128)}, f32[1,1536]{1,0:T(1,128)}) all-reduce(f32[1,2,384]{2,1,0:T(2,128)S(1)} %maximum_bitcast_fusion.6, f32[1,1536]{1,0:T(1,128)S(1)} %stack.144), channel_id=1, replica_groups=mesh['dp'=16,'mp'=2] {'dp'}, use_global_device_ids=true, to_apply=%region_25.26 | all-reduce | flops 2304 | bytes 18432 | tf_op jit(solution)/shard_map/psum | solution.py:431
  987.0 38.5 %all-reduce.11 = (f32[1,3,768]{2,0,1:T(1,128)}, f32[1,3,768]{2,0,1:T(1,128)}, f32[1,3,768]{2,0,1:T(1,128)}, f32[1,2,2,1152]{3,2,1,0:T(2,128)}) all-reduce(f32[1,3,768]{2,0,1:T(1,128)S(1)} %stack.150, f32[1,3,768]{2,0,1:T(1,128)S(1)} %stack.152, f32[1,3,768]{2,0,1:T(1,128)S(1)} %stack.154, ...), channel_id=1, replica_groups=mesh['dp'=16,'mp'=2] {'dp','mp'}, use_global_device_ids=true, to_apply=%region_34.35 | all-reduce | flops 11520 | bytes 92160 | tf_op jit(solution)/shard_map/psum | solution.py:432
  1036.6 51.5 %all-reduce.18.cloned.1.call-done = (f32[512,256]{1,0:T(8,128)}, f32[1,2,256,1152]{3,2,1,0:T(8,128)}, f32[1,2,384,1152]{3,2,1,0:T(8,128)}) async-done(((f32[512,256]{1,0:T(8,128)}, f32[1,2,256,1152]{3,2,1,0:T(8,128)}, f32[1,2,384,1152]{3,2,1,0:T(8,128)}), (f32[512,256]{1,0:T(8,128)}, f32[1,2,256,1152]{3,2,1,0:T(8,128)}, f32[1,2,384,1152]{3,2,1,0:T(8,128)})) %all-reduce.18.cloned.1.call-update) | async-done | bytes 6422544 | tf_op jit(solution)/shard_map/psum | solution.py:432
  1088.1 143.2 %reduce-scatter.15.cloned.1.call-done = f32[1,48,1536]{2,1,0:T(8,128)} async-done(((f32[1,768,1536]{2,1,0:T(8,128)}), f32[1,48,1536]{2,1,0:T(8,128)}) %reduce-scatter.15.cloned.1.call-update) | async-done | bytes 294928 | tf_op jit(solution)/shard_map/reduce_scatter | solution.py:428
  1233.1 3.4 copy.160
  (1360 shorter events, 719.7 us)
Async XLA Ops:
  7.2 161.3 %copy-start = (bf16[1,1536,768]{2,1,0:T(8,128)(2,1)S(1)}, bf16[1,1536,768]{2,1,0:T(8,128)(2,1)}, u32[]{:S(2)}) copy-start(bf16[1,1536,768]{2,1,0:T(8,128)(2,1)} %param.39) | copy-start | bytes 7077892
  7.2 151.2 %reduce-scatter.7.cloned.1.call-start = ((), (), s32[]{:S(2)}) async-start(), calls=%async_computation.6 | async-start | bytes 589824 | tf_op jit(solution)/shard_map/reduce_scatter | solution.py:55
  15.3 4.0 copy-start.37
  15.3 5.1 copy-start.58
  16.7 4.5 copy-start.103
  16.7 5.2 copy-start.83
  20.4 221.5 %reduce-scatter.9.cloned.1.call-start = ((), (), s32[]{:S(2)}) async-start(), calls=%async_computation.7 | async-start | bytes 589824 | tf_op jit(solution)/shard_map/reduce_scatter | solution.py:55
  21.2 139.6 %copy-start.60 = (f32[768]{0:T(1024)}, f32[768]{0:T(1024)S(1)}, u32[]{:S(2)}) copy-start(f32[768]{0:T(1024)S(1)} %get-tuple-element.836) | copy-start | bytes 9220
  25.9 6.2 copy-start.8
  32.1 117.9 %copy-start.91 = (bf16[1,1536]{1,0:T(2,128)(2,1)S(1)}, bf16[1,1536]{1,0:T(2,128)(2,1)}, u32[]{:S(2)}) copy-start(bf16[1,1536]{1,0:T(2,128)(2,1)} %param.38) | copy-start | bytes 9220
  150.7 10.1 copy-start.62
  150.7 10.2 copy-start.68
  159.6 7.7 copy-start.81
  160.8 6.5 copy-start.101
  160.8 6.5 copy-start.84
  170.3 114.5 %reduce-scatter.11.cloned.1.call-start = ((), (), s32[]{:S(2)}) async-start(), calls=%async_computation.8 | async-start | bytes 589824 | tf_op jit(solution)/shard_map/reduce_scatter | solution.py:55
  244.5 9.4 copy-start.18
  244.5 7.0 collective-permute-start.1
  248.0 5.9 copy-start.64
  248.0 5.9 copy-start.80
  248.0 5.9 copy-start.97
  248.0 5.9 collective-permute-start
  251.5 9.2 slice-start.2
  254.0 6.7 slice-start.3
  259.4 3.5 collective-permute-start.3
  261.6 3.1 collective-permute-start.2
  265.6 4.0 copy-start.31
  265.6 4.0 copy-start.110
  272.7 12.1 copy-start.14
  272.7 12.1 copy-start.15
  272.7 12.1 copy-start.17
  272.7 12.1 copy-start.61
  272.7 12.1 copy-start.63
  272.7 12.1 copy-start.82
  272.8 12.1 copy-start.85
  272.8 12.1 copy-start.96
  272.8 14.1 %copy-start.102 = (f32[128]{0:T(128)S(1)}, f32[128]{0:T(128)}, u32[]{:S(2)}) copy-start(f32[128]{0:T(128)} %copy-done.101) | copy-start | bytes 1540
  274.4 751.2 %reduce-scatter.13.cloned.1.call-start = ((), (), s32[]{:S(2)}) async-start(), calls=%async_computation.9 | async-start | bytes 589824 | tf_op jit(solution)/shard_map/reduce_scatter | solution.py:55
  284.9 7.0 copy-start.38
  286.8 7.2 copy-start.7
  291.9 4.0 copy-start.25
  299.3 83.6 %copy-start.41 = (bf16[256,1,384]{2,0,1:T(8,128)(2,1)}, bf16[256,1,384]{2,0,1:T(8,128)(2,1)S(1)}, u32[]{:S(2)}) copy-start(bf16[256,1,384]{2,0,1:T(8,128)(2,1)S(1)} %copy.76) | copy-start | bytes 589828
  299.5 83.4 %copy-start.43 = (bf16[256,1,384]{2,0,1:T(8,128)(2,1)}, bf16[256,1,384]{2,0,1:T(8,128)(2,1)S(1)}, u32[]{:S(2)}) copy-start(bf16[256,1,384]{2,0,1:T(8,128)(2,1)S(1)} %copy.75) | copy-start | bytes 589828
  299.7 83.2 %copy-start.45 = (bf16[256,1,384]{2,0,1:T(8,128)(2,1)}, bf16[256,1,384]{2,0,1:T(8,128)(2,1)S(1)}, u32[]{:S(2)}) copy-start(bf16[256,1,384]{2,0,1:T(8,128)(2,1)S(1)} %copy.74) | copy-start | bytes 589828
  302.7 724.6 %all-reduce.20.cloned.1.call-start = ((), (), s32[]{:S(2)}) async-start(), calls=%async_computation.13 | async-start | bytes 18874368
  370.6 12.3 copy-start.21
  385.4 11.9 copy-start.26
  385.4 11.9 copy-start.48
  400.3 632.1 %reduce-scatter.17.cloned.1.call-start = ((), (), s32[]{:S(2)}) async-start(), calls=%async_computation.11 | async-start | bytes 14598144 | tf_op jit(solution)/shard_map/reduce_scatter | solution.py:436
  402.7 61.1 %copy-start.36 = (bf16[128,384]{1,0:T(8,128)(2,1)S(1)}, bf16[128,384]{1,0:T(8,128)(2,1)}, u32[]{:S(2)}) copy-start(bf16[128,384]{1,0:T(8,128)(2,1)} %convert.31) | copy-start | bytes 294916
  463.8 4.0 copy-start.19
  484.9 603.2 %all-reduce.18.cloned.1.call-start = ((), (), s32[]{:S(2)}) async-start(), calls=%async_computation.12 | async-start | bytes 12845056 | tf_op jit(solution)/shard_map/psum | solution.py:432
  905.8 4.9 copy-start.3
  905.8 4.9 copy-start.34
  912.7 5.5 copy-start.9
  912.7 7.4 slice-start
  927.0 304.2 %reduce-scatter.15.cloned.1.call-start = ((), (), s32[]{:S(2)}) async-start(), calls=%async_computation.10 | async-start | bytes 5013504 | tf_op jit(solution)/shard_map/reduce_scatter | solution.py:428
  937.4 4.0 copy-start.76
  937.4 4.0 copy-start.74
  937.4 4.1 copy-start.42
  937.5 4.1 copy-start.44
  937.5 4.1 copy-start.46
  937.5 88.1 %copy-start.24 = (f32[128,768]{1,0:T(8,128)S(1)}, f32[128,768]{1,0:T(8,128)}, u32[]{:S(2)}) copy-start(f32[128,768]{1,0:T(8,128)} %copy-done.23) | copy-start | bytes 1179652
  937.5 88.1 %copy-start.99 = (f32[128]{0:T(128)S(1)}, f32[128]{0:T(128)}, u32[]{:S(2)}) copy-start(f32[128]{0:T(128)} %copy-done.98) | copy-start | bytes 1540
  (120 other events, 285.6 us)
Sparse Core Ops, SparseCore 0:
  20.6 10.3 reduce-scatter.6
  170.4 10.3 reduce-scatter.8
  274.5 10.3 reduce-scatter.10
  302.8 8.9 reduce-scatter.12
  400.4 283.2 all-reduce.19
  689.6 161.9 reduce-scatter.16
  927.1 160.8 all-reduce.17
  1093.8 137.3 reduce-scatter.14
where the time goes:
time: 1270 us; the launch traced here: 1250 us
  matrix products  403 us (32%)
  other arithmetic  308 us (24%)
  local copies, waits for them, and re-layouts  206 us (16%)
  waiting for transfers between devices  206 us (16%)
  blocking collectives  94.7 us (7%)
  between operations  17 us (1%)
    reduce_scatter x1, waiting for transfers between devices, per_device(): lax.psum_scatter(merged[3], 'dp', scatter_dimension=1, tiled=True)  143 us
    squeeze x120, local copies, waits for them, and re-layouts, gru_run(): lax.scan(advance, initial, (drive_all, char_mask), reverse=direction == 1)  134 us
    dot_general x40, matrix products, retreat(): jnp.dot(prior_low.T, recur_low, preferred_element_type=jnp.float32)  133 us
    dot_general x80, matrix products, advance(): jnp.dot(carried.astype(jnp.bfloat16), hid_matrix, preferred_element_type=...  84.6 us
    sub x120, other arithmetic, gate_apply(): return mask_step * moved + (1.0 - mask_step) * carried  79.4 us
    psum x1, waiting for transfers between devices, per_device(): lax.psum((merged[6], merged[7], merged[8], table_grad, merged[9], merged[...  51.5 us
    dot_general x40, matrix products, retreat(): jnp.dot(recur_low, hid_matrix.T, preferred_element_type=jnp.float32)  51.4 us
    dot_general x40, matrix products, retreat(): jnp.dot(prior_low, hid_matrix, preferred_element_type=jnp.float32)  51.1 us
  transfers between devices with their start and end apart: 12, of which 4 were waited for; matrix products, arithmetic and copies ran while one was open for 68% of the time, Pallas kernels for 0%

commit v1 on v0

v1 whole, which is shorter than its diff:
```python
import jax
import jax.numpy as jnp
from jax import lax
from jax.experimental import pallas as pl
from jax.experimental.pallas import tpu as pltpu
from jax.sharding import PartitionSpec as P

HD = 64
EPSILON = 1e-05
bf16 = jnp.bfloat16
f32 = jnp.float32


def dot(left, right):
    return jnp.dot(left, right, preferred_element_type=f32)


def dot_t(left, right):
    return lax.dot_general(left, right, (((0,), (0,)), ((), ())), preferred_element_type=f32)


def dot_r(left, right):
    return lax.dot_general(left, right, (((1,), (1,)), ((), ())), preferred_element_type=f32)


def sigmoid(x):
    return 0.5 * jnp.tanh(0.5 * x) + 0.5


def gru_fwd_kernel(ef, eb, lens, win, whid, bias, c_ref, cof, chf, hpf, cob, chb, hpb, h_ref):
    s = pl.program_id(0)
    n = pl.num_programs(0)
    gh = h_ref.shape[2]

    @pl.when(s == 0)
    def _():
        h_ref[...] = jnp.zeros_like(h_ref)

    for d, (e, co, ch, hp) in enumerate(((ef, cof, chf, hpf), (eb, cob, chb, hpb))):
        slot = s if d == 0 else n - 1 - s
        mask = (slot < lens[...]).astype(f32)
        h = h_ref[d]
        low = h.astype(bf16)
        g = dot(e[0], win[d]) + bias[2 * d : 2 * d + 1]
        y = dot(low, whid[d]) + bias[2 * d + 1 : 2 * d + 2]
        r = sigmoid(g[:, :gh] + y[:, :gh])
        z = sigmoid(g[:, gh : 2 * gh] + y[:, gh : 2 * gh])
        yn = y[:, 2 * gh :]
        fresh = jnp.tanh(g[:, 2 * gh :] + r * yn)
        keep = mask * (1.0 - z)
        moved = keep * (h - fresh)
        h_ref[d] = h - moved
        an = keep * (1.0 - fresh * fresh)
        ay = an * r
        ar = ay * yn * (1.0 - r)
        co[0, :, 0:gh] = ay.astype(bf16)
        co[0, :, gh : 2 * gh] = ar.astype(bf16)
        co[0, :, 2 * gh : 3 * gh] = (moved * z).astype(bf16)
        co[0, :, 3 * gh :] = an.astype(bf16)
        ch[0] = 1.0 - keep
        hp[0] = low

    @pl.when(s == n - 1)
    def _():
        c_ref[:, :gh] = h_ref[0].astype(bf16)
        c_ref[:, gh:] = h_ref[1].astype(bf16)


def gru_fwd(emb, lens, win, whid, bias):
    slots, rows, width = emb.shape
    gh = whid.shape[1]
    fw = lambda s: (s, 0, 0)
    bw = lambda s: (slots - 1 - s, 0, 0)
    blk = lambda w, im: pl.BlockSpec((1, rows, w), im)
    full = lambda a: pl.BlockSpec(a.shape, lambda s: (0,) * a.ndim)
    sd = jax.ShapeDtypeStruct
    return pl.pallas_call(
        gru_fwd_kernel,
        grid=(slots,),
        in_specs=[blk(width, fw), blk(width, bw), full(lens), full(win), full(whid), full(bias)],
        out_specs=[pl.BlockSpec((rows, 2 * gh), lambda s: (0, 0))]
        + [blk(4 * gh, fw), blk(gh, fw), blk(gh, fw), blk(4 * gh, bw), blk(gh, bw), blk(gh, bw)],
        out_shape=[sd((rows, 2 * gh), bf16)]
        + [sd((slots, rows, 4 * gh), bf16), sd((slots, rows, gh), f32), sd((slots, rows, gh), bf16)] * 2,
        scratch_shapes=[pltpu.VMEM((2, rows, gh), f32)],
        compiler_params=pltpu.CompilerParams(vmem_limit_bytes=32 << 20),
        cost_estimate=pl.CostEstimate(flops=1 << 20, bytes_accessed=1 << 10, transcendentals=0),
        name="gru_fwd",
    )(emb, emb, lens, win, whid, bias)


def gru_bwd_kernel(dc, wht, cof, chf, cob, chb, gf, gb, bs_ref, dh_ref, acc):
    i = pl.program_id(0)
    n = pl.num_programs(0)
    gh = dh_ref.shape[2]

    @pl.when(i == 0)
    def _():
        dh_ref[0] = dc[:, :gh]
        dh_ref[1] = dc[:, gh:]
        acc[...] = jnp.zeros_like(acc)

    for d, (co, ch, g) in enumerate(((cof, chf, gf), (cob, chb, gb))):
        dh = dh_ref[d]
        parts = [dh * co[0, :, k * gh : (k + 1) * gh].astype(f32) for k in range(4)]
        low = [p.astype(bf16) for p in parts]
        for k in range(4):
            g[0, :, k * gh : (k + 1) * gh] = low[k]
            acc[d, :, k * gh : (k + 1) * gh] += parts[k].reshape(-1, 8, gh).sum(0)
        dy = jnp.concatenate(low[:3], 1)
        dh_ref[d] = dh * ch[0] + dot(dy, wht[d])

    @pl.when(i == n - 1)
    def _():
        bs_ref[...] = acc[...].sum(1)


def gru_bwd(dc, wht, cof, chf, cob, chb):
    slots, rows, gh = chf.shape
    fw = lambda s: (slots - 1 - s, 0, 0)
    bw = lambda s: (s, 0, 0)
    blk = lambda w, im: pl.BlockSpec((1, rows, w), im)
    full = lambda a: pl.BlockSpec(a.shape, lambda s: (0,) * a.ndim)
    sd = jax.ShapeDtypeStruct
    return pl.pallas_call(
        gru_bwd_kernel,
        grid=(slots,),
        in_specs=[full(dc), full(wht), blk(4 * gh, fw), blk(gh, fw), blk(4 * gh, bw), blk(gh, bw)],
        out_specs=[blk(4 * gh, fw), blk(4 * gh, bw), pl.BlockSpec((2, 4 * gh), lambda s: (0, 0))],
        out_shape=[sd((slots, rows, 4 * gh), bf16)] * 2 + [sd((2, 4 * gh), f32)],
        scratch_shapes=[pltpu.VMEM((2, rows, gh), f32), pltpu.VMEM((2, 8, 4 * gh), f32)],
        compiler_params=pltpu.CompilerParams(vmem_limit_bytes=32 << 20),
        cost_estimate=pl.CostEstimate(flops=1 << 20, bytes_accessed=1 << 10, transcendentals=0),
        name="gru_bwd",
    )(dc, wht, cof, chf, cob, chb)


GELU_A = 0.7978845608028654
GELU_B = 0.044715


def norm_stats(total):
    centre = jnp.mean(total, -1, keepdims=True)
    centred = total - centre
    scale = lax.rsqrt(jnp.mean(centred * centred, -1, keepdims=True) + EPSILON)
    return centred * scale, scale


def norm_back(grad, hat, scale, gain):
    scaled = grad * gain
    inner = jnp.mean(scaled, -1, keepdims=True)
    along = jnp.mean(scaled * hat, -1, keepdims=True)
    return (scaled - inner - hat * along) * scale


def gelu_pair(u):
    square = u * u
    t = jnp.tanh(GELU_A * (u + GELU_B * u * square))
    half = 0.5 * (1.0 + t)
    slope = half + 0.5 * u * (1.0 - t * t) * (GELU_A + 3.0 * GELU_A * GELU_B * square)
    return u * half, slope


def turned(values):
    rows = values.shape[0] // 2
    return jnp.concatenate([values[rows:], values[:rows]], 0)


def own_sum(values):
    return jnp.sum(values[: values.shape[0] // 2], 0, keepdims=True)


def pair_of(left, right):
    return jnp.concatenate([left, right], 0)


class Halves:
    def __init__(self, length, bit):
        self.count = lax.axis_size("dp")
        self.length, self.bit = length, bit
        self.chunk = length // self.count
        self.direct = self.chunk % 16 == 0

    def operands(self):
        if self.direct:
            return []
        mine = (lax.axis_index("dp") >> self.bit) & 1
        where = jnp.arange(self.length, dtype=jnp.int32)
        kept = where.reshape(self.count >> (self.bit + 1), 2, -1)
        pick = lambda side: jax.nn.one_hot(
            lax.dynamic_index_in_dim(kept, side, 1, keepdims=False).reshape(-1), self.length, dtype=bf16
        )
        return [pick(1 - mine), pick(mine)]

    def scratch(self, rows):
        return [pltpu.VMEM((self.length, rows), bf16)]

    def sides(self, values, turned_ref, place, picks):
        if not self.direct:
            return [dot_r(pick[...], values).astype(bf16) for pick in picks]
        turned_ref[...] = values.T
        mine = (place[0] >> self.bit) & 1
        out = []
        for side in (1 - mine, mine):
            parts = []
            for k in range(self.count):
                if not (k >> self.bit) & 1:
                    start = pl.multiple_of((k + (side << self.bit)) * self.chunk, 16)
                    parts.append(turned_ref[pl.ds(start, self.chunk), :])
            out.append(jnp.concatenate(parts, 0))
        return out


VMEM = pl.BlockSpec(memory_space=pltpu.VMEM)
SMEM = pl.BlockSpec(memory_space=pltpu.SMEM)


def whole_call(kernel, args, outs, scratch, limit, flops, name):
    return pl.pallas_call(
        kernel,
        in_specs=[SMEM] + [VMEM] * (len(args) - 1),
        out_specs=[VMEM] * len(outs),
        out_shape=[jax.ShapeDtypeStruct(*o) for o in outs],
        scratch_shapes=scratch,
        compiler_params=pltpu.CompilerParams(vmem_limit_bytes=limit << 20),
        cost_estimate=pl.CostEstimate(flops=1 << 20, bytes_accessed=1 << 10, transcendentals=0),
        name=name,
    )(*args)


def attend_fwd(place, mine, other, wqkv, bqkv, wout, vec, q_ref, k_ref, v_ref, p_ref, m_ref, base_ref, send_ref):
    x = pair_of(mine[...], other[...])
    bias = bqkv[...].astype(f32)
    q = (dot(x, wqkv[0]) + bias[0:1]).astype(bf16)
    k = dot(x, wqkv[1]).astype(bf16)
    v = (dot(x, wqkv[2]) + bias[1:2]).astype(bf16)
    q_ref[...], k_ref[...], v_ref[...] = q, k, v
    mixed = []
    for h in range(p_ref.shape[0]):
        at = slice(h * HD, (h + 1) * HD)
        s = dot_r(q[:, at], k[:, at]) * HD**-0.5
        e = jnp.exp(s - jnp.max(s, -1, keepdims=True))
        p = (e / jnp.sum(e, -1, keepdims=True)).astype(bf16)
        p_ref[h] = p
        mixed.append(dot(p, v[:, at]).astype(bf16))
    mixed = jnp.concatenate(mixed, 1)
    m_ref[...] = mixed
    part = dot(mixed, wout[...])
    send_ref[...] = part.astype(bf16)
    base_ref[...] = x.astype(f32) + part + vec[0:1]


def feed_fwd(place, base, got, wup, bup, wdown, vec, hat_ref, scale_ref, act_ref, slope_ref, out_ref, send_ref):
    hat, scale = norm_stats(base[...] + turned(got[...]).astype(f32))
    hat_ref[...], scale_ref[...] = hat, scale
    h1 = hat * vec[3:4] + vec[6:7]
    act, slope = gelu_pair(dot(h1.astype(bf16), wup[...]) + bup[...].astype(f32))
    act = act.astype(bf16)
    act_ref[...] = act
    slope_ref[...] = slope.astype(bf16)
    part = dot(act, wdown[...])
    send_ref[...] = part.astype(bf16)
    out_ref[...] = h1 + part + vec[1:2]


def unite(halves, place, base, got, cm, co, conv, tm, to, vec, *rest):
    picks, rest = rest[: 0 if halves.direct else 2], rest[0 if halves.direct else 2 :]
    res_ref, dc_ref, dr_ref, sums_ref, gone_ref, kept_ref, turned_ref, cat_ref = rest
    core = place[1]
    hat2, scale2 = norm_stats(base[...] + turned(got[...]).astype(f32))
    h2 = hat2 * vec[4:5] + vec[7:8]
    joined = jnp.concatenate([h2.astype(bf16), pair_of(cm[...], co[...])], 1)
    rows = joined.shape[0]
    width = h2.shape[1]
    spot = lax.broadcasted_iota(jnp.int32, (rows, 1), 0)
    half = rows // 2
    not_first = (spot != core * half).astype(f32)
    not_last = (spot != (rows - 1 + core * half) % rows).astype(f32)
    later = lambda a: pltpu.roll(a, 1, 0) * not_first
    sooner = lambda a: pltpu.roll(a, rows - 1, 0) * not_last
    raw = later(dot(joined, conv[0])) + dot(joined, conv[1]) + sooner(dot(joined, conv[2])) + vec[2:3]
    act, slope = gelu_pair(raw)
    hat3, scale3 = norm_stats(h2 + act)
    res_ref[...] = (hat3 * vec[5:6] + vec[8:9])[:half].astype(bf16)
    cot = pair_of(tm[...], to[...]).astype(f32)
    d_r3 = norm_back(cot, hat3, scale3, vec[5:6])
    d_f = (d_r3 * slope).astype(bf16).astype(f32)
    d_fs = [sooner(d_f).astype(bf16), d_f.astype(bf16), later(d_f).astype(bf16)]
    d_h2 = d_r3 + sum(dot_r(d_fs[i], conv[i, :width]) for i in range(3))
    dc_ref[...] = sum(dot_r(d_fs[i][:half], conv[i, width:]) for i in range(3))
    d_r2 = norm_back(d_h2, hat2, scale2, vec[4:5])
    dr_ref[...] = d_r2
    sums = [own_sum(d_r2), own_sum(d_f), own_sum(d_h2 * hat2), own_sum(cot * hat3), own_sum(d_h2), own_sum(cot)]
    for i, value in enumerate(sums):
        sums_ref[i : i + 1] = value
    span = width // 2
    for i in range(3):
        cat_ref[i] = d_fs[i]
        part = cat_ref[i, :, pl.ds(pl.multiple_of(core * span, 128), span)]
        if i == 0:
            gone, kept = halves.sides(joined, turned_ref, place, picks)
        gone_ref[:, i * span : (i + 1) * span] = dot(gone, part).astype(bf16)
        kept_ref[:, i * span : (i + 1) * span] = dot(kept, part).astype(bf16)


def feed_back(halves, place, dr, act, slope, hat, wup, wdown, vec, *rest):
    picks, rest = rest[: 0 if halves.direct else 2], rest[0 if halves.direct else 2 :]
    base_ref, send_ref, sum_ref, gone_ref, kept_ref, turned_ref = rest
    low = dr[...].astype(bf16)
    d_u = (dot_r(low, wdown[...]) * slope[...].astype(f32)).astype(bf16)
    sum_ref[...] = jnp.sum(d_u.astype(f32), 0, keepdims=True)
    part = dot_r(d_u, wup[...])
    send_ref[...] = part.astype(bf16)
    base_ref[...] = dr[...] + part
    h1 = (hat[...] * vec[3:4] + vec[6:7]).astype(bf16)
    span = d_u.shape[1]
    for place_, (left, right) in enumerate(((h1, d_u), (low, act[...]))):
        gone, kept = halves.sides(left, turned_ref, place, picks)
        gone_ref[:, place_ * span : (place_ + 1) * span] = dot(gone, right).astype(bf16)
        kept_ref[:, place_ * span : (place_ + 1) * span] = dot(kept, right).astype(bf16)


def attend_back(halves, place, base, got, hat, scale, q, k, v, p, mixed, mine, other, wqkv, wout, vec, *rest):
    picks, rest = rest[: 0 if halves.direct else 2], rest[0 if halves.direct else 2 :]
    base_ref, send_ref, sums_ref, shift_ref, gone_ref, kept_ref, turned_ref = rest
    d_h1 = base[...] + turned(got[...]).astype(f32)
    d_r1 = norm_back(d_h1, hat[...], scale[...], vec[3:4])
    for i, value in enumerate((own_sum(d_r1), own_sum(d_h1 * hat[...]), own_sum(d_h1))):
        sums_ref[i : i + 1] = value
    low = d_r1.astype(bf16)
    d_mixed = dot_r(low, wout[...]).astype(bf16)
    d_q, d_k, d_v = [], [], []
    for h in range(p.shape[0]):
        at = slice(h * HD, (h + 1) * HD)
        prob = p[h].astype(f32)
        d_p = dot_r(d_mixed[:, at], v[:, at])
        d_v.append(dot_t(p[h], d_mixed[:, at]).astype(bf16))
        d_s = (prob * (d_p - jnp.sum(prob * d_p, -1, keepdims=True))).astype(bf16)
        d_q.append((dot(d_s, k[:, at]) * HD**-0.5).astype(bf16))
        d_k.append((dot_t(d_s, q[:, at]) * HD**-0.5).astype(bf16))
    d_proj = [jnp.concatenate(a, 1) for a in (d_q, d_k, d_v)]
    shift_ref[0:1] = jnp.sum(d_proj[0].astype(f32), 0, keepdims=True)
    shift_ref[1:2] = jnp.sum(d_proj[2].astype(f32), 0, keepdims=True)
    part = sum(dot_r(d_proj[i], wqkv[i]) for i in range(3))
    rows = part.shape[0] // 2
    base_ref[...] = d_r1[:rows] + part[:rows]
    send_ref[...] = part[rows:].astype(bf16)
    span = d_mixed.shape[1]
    x = pair_of(mine[...], other[...])
    gone, kept = halves.sides(x, turned_ref, place, picks)
    for i in range(3):
        gone_ref[:, i * span : (i + 1) * span] = dot(gone, d_proj[i]).astype(bf16)
        kept_ref[:, i * span : (i + 1) * span] = dot(kept, d_proj[i]).astype(bf16)
    gone, kept = halves.sides(low, turned_ref, place, picks)
    gone_ref[:, 3 * span :] = dot(gone, mixed[...]).astype(bf16)
    kept_ref[:, 3 * span :] = dot(kept, mixed[...]).astype(bf16)


class Packing:
    def __init__(self, width, embed, gh, vocab):
        self.width, self.embed, self.gh, self.vocab = width, embed, gh, vocab
        self.groups = 6 * gh // width
        self.per_row = width // embed
        self.long = -(-vocab // (16 * self.per_row)) * 16
        self.hid_at = self.groups * embed
        self.table_at = self.hid_at + self.groups * gh
        self.small_at = self.table_at + self.long
        unit = 16 * lax.axis_size("dp")
        if lax.axis_size("dp") % 8 == 0:
            unit = 8 * lax.axis_size("dp")
        self.rows = -(-(self.small_at + 32) // unit) * unit
        self.half = self.rows // 2


def put(pack, core, kept_ref, gone_ref, at, value):
    rows = value.shape[0]
    cuts = [(max(at, h * pack.half), min(at + rows, (h + 1) * pack.half), h) for h in range(2)]
    for low, high, h in cuts:
        if high > low:
            piece = value[low - at : high - at].astype(bf16)
            where = slice(low - h * pack.half, high - h * pack.half)

            @pl.when(core == h)
            def _(piece=piece, where=where):
                kept_ref[where] = piece

            @pl.when(core != h)
            def _(piece=piece, where=where):
                gone_ref[where] = piece


def gru_weights(pack, place, gf, gb, hpf, hpb, emb, ids, win, small, kept_ref, gone_ref, hid_acc, in_acc, table_acc):
    i = pl.program_id(0)
    gh = hpf.shape[-1]
    flat = lambda ref: ref[...].reshape(-1, ref.shape[-1])

    @pl.when(i == 0)
    def _():
        hid_acc[...] = jnp.zeros_like(hid_acc)
        in_acc[...] = jnp.zeros_like(in_acc)
        table_acc[...] = jnp.zeros_like(table_acc)

    e = flat(emb)
    d_e = 0.0
    for d, (g, before) in enumerate(((gf, hpf), (gb, hpb))):
        grads = flat(g)
        hid_acc[d] += dot_t(flat(before), grads[:, : 3 * gh])
        in_acc[d] += dot_t(e, grads[:, gh:])
        d_e = d_e + dot_r(grads[:, gh:], win[d])
    chosen = lax.broadcasted_iota(jnp.int32, (pack.vocab, e.shape[0]), 0) == ids[0]
    table_acc[...] += dot(chosen.astype(bf16), d_e.astype(bf16))

    @pl.when(i == pl.num_programs(0) - 1)
    def _():
        core = place[1]
        store = lambda at, value: put(pack, core, kept_ref, gone_ref, at, value)
        whole = jnp.concatenate([in_acc[0], in_acc[1]], 1)
        for g in range(pack.groups):
            store(g * pack.embed, whole[:, g * pack.width : (g + 1) * pack.width])
        whole = jnp.concatenate(
            [a for d in range(2) for a in (hid_acc[d, :, gh:], hid_acc[d, :, :gh])], 1
        )
        for g in range(pack.groups):
            store(pack.hid_at + g * gh, whole[:, g * pack.width : (g + 1) * pack.width])
        parts = []
        for g in range(pack.per_row):
            part = table_acc[g * pack.long : min((g + 1) * pack.long, pack.vocab)]
            short = pack.long - part.shape[0]
            if short:
                part = jnp.concatenate([part, jnp.zeros((short, pack.embed), f32)], 0)
            parts.append(part)
        store(pack.table_at, jnp.concatenate(parts, 1))
        store(pack.small_at, small[...])


def gru_pack(pack, place, gf, gb, hpf, hpb, emb, ids, win, small, step):
    slots, rows, gh = hpf.shape
    count = slots // step
    blk = lambda a: pl.BlockSpec((step,) + a.shape[1:], lambda i: (i, 0, 0))
    full = lambda a: pl.BlockSpec(a.shape, lambda i: (0,) * a.ndim)
    out = jax.ShapeDtypeStruct((pack.half, pack.width), bf16)
    return pl.pallas_call(
        lambda *refs: gru_weights(pack, *refs),
        grid=(count,),
        in_specs=[SMEM]
        + [blk(a) for a in (gf, gb, hpf, hpb, emb)]
        + [pl.BlockSpec((1, 1, step * rows), lambda i: (i, 0, 0)), full(win), full(small)],
        out_specs=[pl.BlockSpec((pack.half, pack.width), lambda i: (0, 0))] * 2,
        out_shape=[out, out],
        scratch_shapes=[
            pltpu.VMEM((2, gh, 3 * gh), f32),
            pltpu.VMEM((2, pack.embed, 3 * gh), f32),
            pltpu.VMEM((pack.vocab, pack.embed), f32),
        ],
        compiler_params=pltpu.CompilerParams(vmem_limit_bytes=48 << 20),
        cost_estimate=pl.CostEstimate(flops=1 << 20, bytes_accessed=1 << 10, transcendentals=0),
        name="gru_pack",
    )(place, gf, gb, hpf, hpb, emb, ids.reshape(count, 1, step * rows), win, small)


def unpack(pack, place, own, got, in_ref, hid_ref, table_ref, small_ref, all_ref):
    core = place[1]
    start = pl.multiple_of(core * pack.half, 16)
    all_ref[pl.ds(start, pack.half), :] = own[...]
    start = pl.multiple_of((1 - core) * pack.half, 16)
    all_ref[pl.ds(start, pack.half), :] = got[...]
    gh, width = pack.gh, pack.width
    for at, length, ref in ((0, pack.embed, in_ref), (pack.hid_at, gh, hid_ref)):
        for g in range(pack.groups):
            piece = all_ref[at + g * length : at + (g + 1) * length].astype(f32)
            for d in range(2):
                low, high = max(g * width, d * 3 * gh), min((g + 1) * width, (d + 1) * 3 * gh)
                if high > low:
                    ref[d, :, low - d * 3 * gh : high - d * 3 * gh] = piece[:, low - g * width : high - g * width]
    for g in range(pack.per_row):
        count = min((g + 1) * pack.long, pack.vocab) - g * pack.long
        piece = all_ref[pack.table_at : pack.table_at + count, g * pack.embed : (g + 1) * pack.embed]
        table_ref[g * pack.long : g * pack.long + count] = piece.astype(f32)
    small_ref[...] = all_ref[pack.small_at : pack.small_at + 32].astype(f32)


def swap(values):
    return lax.ppermute(values, "mp", [(0, 1), (1, 0)])


def flip(values, bit):
    count = lax.axis_size("dp")
    return lax.ppermute(values, "dp", [(i, i ^ (1 << bit)) for i in range(count)])


def bit_of(bit):
    return (lax.axis_index("dp") >> bit) & 1


def added(left, right, dtype=bf16):
    return (left.astype(f32) + right.astype(f32)).astype(dtype)


def reduce_rows(gone, kept, order, last=f32):
    count = lax.axis_size("dp")
    bits = count.bit_length() - 1
    held = [bit for bit in range(bits)[::-1] if bit != order[0]]
    shape = (2,) * (bits - 1) + (kept.shape[0] * 2 // count, kept.shape[1])
    got = flip(gone, order[0]).reshape(shape)
    kept = kept.reshape(shape)
    for bit in order[1:]:
        axis = held.index(bit)
        side = lambda a, index: lax.dynamic_index_in_dim(a, index, axis, keepdims=False)
        mine = bit_of(bit)
        gone = added(side(kept, 1 - mine), side(got, 1 - mine))
        kept = added(side(kept, mine), side(got, mine))
        got = flip(gone, bit)
        held.pop(axis)
    return added(kept, got, last)


def all_sum(block, order):
    dims = []
    for bit in order:
        dim = 0 if block.shape[0] % 16 == 0 else 1
        dims.append(dim)
        size = block.shape[dim] // 2
        side = lambda index: lax.dynamic_slice_in_dim(block, index * size, size, dim)
        mine = bit_of(bit)
        block = added(side(mine), flip(side(1 - mine), bit))
    for bit, dim in zip(order[::-1], dims[::-1]):
        got = flip(block, bit)
        block = jnp.where(
            bit_of(bit) == 0, jnp.concatenate([block, got], dim), jnp.concatenate([got, block], dim)
        )
    return block


def per_device(
    tokens,
    cotangent,
    char_ids,
    char_lens,
    w_qkv,
    b_qkv,
    w_out,
    w_up,
    up_bias,
    w_down,
    res_bias,
    norm_gain,
    norm_bias,
    char_table,
    gru_in,
    gru_hid,
    gru_bias,
    conv_w,
):
    core = lax.axis_index("mp")
    place = jnp.stack([lax.axis_index("dp"), core]).astype(jnp.int32)
    rows, width = tokens.shape
    both = 2 * rows
    slots = char_ids.shape[1]
    vocab, embed = char_table.shape
    gh = gru_hid.shape[2]
    bits = list(range(lax.axis_size("dp").bit_length() - 1))
    order_a = bits
    order_b = bits[1::-1] + bits[2:]
    order_c = bits[2:3] + bits[:2] + bits[3:]
    wqkv = w_qkv[0].swapaxes(0, 1)
    cols = wqkv.shape[2]
    wout, wup, wdown, conv = w_out[0], w_up[0], w_down[0], conv_w[0]
    units = wup.shape[1]
    vec = jnp.concatenate([res_bias[0], norm_gain[0], norm_bias[0]], 0).astype(f32)
    heads = cols // HD

    tokens_other = swap(tokens)
    cot_other = swap(cotangent)

    ids = char_ids.T.reshape(-1)
    one_hot = (ids[:, None] == jnp.arange(vocab, dtype=jnp.int32)[None, :]).astype(bf16)
    emb = dot(one_hot, char_table).astype(bf16).reshape(slots, rows, embed)
    chars, cof, chf, hpf, cob, chb, hpb = gru_fwd(
        emb, char_lens[:, None], gru_in[0], gru_hid[0], gru_bias[0].astype(f32).reshape(4, -1)
    )
    chars_other = swap(chars)

    q, k, v, p, mixed, base, send = whole_call(
        attend_fwd,
        (place, tokens, tokens_other, wqkv, b_qkv[0], wout, vec),
        [((both, cols), bf16)] * 3
        + [((heads, both, both), bf16), ((both, cols), bf16), ((both, width), f32), ((both, width), bf16)],
        [],
        24,
        2 << 30,
        "attend_fwd",
    )
    hat1, scale1, act, slope, base, send = whole_call(
        feed_fwd,
        (place, base, swap(send), wup, up_bias, wdown, vec),
        [((both, width), f32), ((both, 1), f32), ((both, units), bf16), ((both, units), bf16)]
        + [((both, width), f32), ((both, width), bf16)],
        [],
        24,
        2 << 30,
        "feed_fwd",
    )
    halves = Halves(2 * width, order_a[0])
    span = 3 * width // 2
    result, d_chars, d_r2, sums_b, gone, kept = whole_call(
        lambda *refs: unite(halves, *refs),
        (place, base, swap(send), chars, chars_other, conv, cotangent, cot_other, vec, *halves.operands()),
        [((rows, width), bf16), ((rows, width), f32), ((both, width), f32), ((6, width), f32)]
        + [((width, span), bf16)] * 2,
        halves.scratch(both) + [pltpu.VMEM((3, both, width), bf16)],
        32,
        4 << 30,
        "unite",
    )
    kernel = reduce_rows(gone, kept, order_a, bf16)

    halves = Halves(width, order_b[0])
    base, send, up_shift, gone, kept = whole_call(
        lambda *refs: feed_back(halves, *refs),
        (place, d_r2, act, slope, hat1, wup, wdown, vec, *halves.operands()),
        [((both, width), f32), ((both, width), bf16), ((1, units), f32)] + [((width // 2, 2 * units), bf16)] * 2,
        halves.scratch(both),
        24,
        4 << 30,
        "feed_back",
    )
    feed_grad = reduce_rows(gone, kept, order_b)

    halves = Halves(width, order_c[0])
    base, send, sums_a, q_shift, gone, kept = whole_call(
        lambda *refs: attend_back(halves, *refs),
        (place, base, swap(send), hat1, scale1, q, k, v, p, mixed, tokens, tokens_other, wqkv, wout, vec)
        + tuple(halves.operands()),
        [((rows, width), f32), ((rows, width), bf16), ((3, width), f32), ((2, cols), f32)]
        + [((width // 2, 4 * cols), bf16)] * 2,
        halves.scratch(both),
        24,
        4 << 30,
        "attend_back",
    )
    tokens_grad = base + swap(send).astype(f32)
    attend_grad = reduce_rows(gone, kept, order_c)

    hid = gru_hid[0]
    hid_t = jnp.concatenate([hid[:, :, 2 * gh :], hid[:, :, : 2 * gh]], 2).transpose(0, 2, 1)
    g_f, g_b, sums = gru_bwd(d_chars, hid_t, cof, chf, cob, chb)

    side = jnp.concatenate([q_shift.reshape(1, -1), up_shift], 1).reshape(-1, width)
    zero = jnp.zeros_like(side)
    shifts = [jnp.concatenate([sums[d, gh:], sums[d, gh : 3 * gh], sums[d, :gh]]) for d in range(2)]
    small = jnp.concatenate(
        [
            sums_a[0:1],
            sums_b[0:2],
            sums_a[1:2],
            sums_b[2:4],
            sums_a[2:3],
            sums_b[4:6],
            jnp.concatenate(shifts).reshape(-1, width),
            jnp.where(core == 0, side, zero),
            jnp.where(core == 1, side, zero),
        ],
        0,
    )
    small = jnp.pad(small, ((0, 32 - small.shape[0]), (0, 0)))
    pack = Packing(width, embed, gh, vocab)
    kept, gone = gru_pack(pack, place, g_f, g_b, hpf, hpb, emb, ids, gru_in[0], small, 4)
    own = all_sum(added(kept, swap(gone)), order_a)
    in_out, hid_out, table_out, small = whole_call(
        lambda *refs: unpack(pack, *refs),
        (place, own, swap(own)),
        [((2, embed, 3 * gh), f32), ((2, gh, 3 * gh), f32), ((vocab, embed), f32), ((32, width), f32)],
        [pltpu.VMEM((pack.rows, width), bf16)],
        32,
        1 << 20,
        "unpack",
    )
    res_out, gain_out, offset_out = small[:9].reshape(3, 1, 3, width)
    shift_out = small[9:15].reshape(1, 2, 2, 3 * gh)
    sides = lax.dynamic_slice_in_dim(small, 15 + core * side.shape[0], side.shape[0], 0).reshape(-1)
    kernel_other = swap(kernel)
    low = jnp.where(core == 0, kernel, kernel_other)
    high = jnp.where(core == 0, kernel_other, kernel)
    cut = width // 2
    kernel = jnp.stack(
        [jnp.concatenate([a[:, i * cut : (i + 1) * cut] for a in (low, high)], 1) for i in range(3)]
    ).astype(f32)
    qkv_grad = jnp.stack([attend_grad[:, i * cols : (i + 1) * cols] for i in range(3)], 1)
    return (
        result,
        tokens_grad,
        qkv_grad[None],
        sides[: 2 * cols].reshape(1, 2, cols),
        attend_grad[:, 3 * cols :].T[None],
        feed_grad[:, :units][None],
        sides[2 * cols :][None],
        feed_grad[:, units:].T[None],
        res_out,
        gain_out,
        offset_out,
        table_out,
        in_out[None],
        hid_out[None],
        shift_out,
        kernel[None],
    )


def solution(mesh):
    return jax.shard_map(
        per_device,
        mesh=mesh,
        in_specs=(
            P(("dp", "mp"), None),
            P(("dp", "mp"), None),
            P(("dp", "mp"), None),
            P(("dp", "mp")),
            P(None, None, None, "mp"),
            P(None, None, "mp"),
            P(None, "mp", None),
            P(None, None, "mp"),
            P(None, "mp"),
            P(None, "mp", None),
            P(),
            P(),
            P(),
            P(),
            P(),
            P(),
            P(),
            P(),
        ),
        out_specs=(
            P(("dp", "mp"), None),
            P(("dp", "mp"), None),
            P(None, "dp", None, "mp"),
            P(None, None, "mp"),
            P(None, "mp", "dp"),
            P(None, "dp", "mp"),
            P(None, "mp"),
            P(None, "mp", "dp"),
            P(),
            P(),
            P(),
            P(),
            P(),
            P(),
            P(),
            P(None, None, "dp", None),
        ),
        check_vma=False,
    )
```

time: 1270 us -> 331 us (0.26); the launches traced: 1250 us -> 329 us
  matrix products: 403 us -> 1.64 us
  other arithmetic: 308 us -> 18.2 us
  local copies, waits for them, and re-layouts: 206 us -> 62 us
  blocking collectives: 94.7 us -> 0 us
  Pallas kernels: 0 us -> 92.4 us
  waiting for transfers between devices: 206 us -> 122 us
  starting transfers between devices: 8.12 us -> 31 us
  between operations: 17 us -> 1.28 us
    dot_general x235 -> x1, matrix products: 403 us -> 1.64 us  [dot(): return jnp.dot(left, right, preferred_element_type=f32)]
    reduce_scatter x6 -> x0, waiting for transfers between devices: 154 us -> none  [the longest x1 143 us: per_device(): lax.psum_scatter(merged[3], 'dp', scatter_dimension=1, tiled=True)]
    squeeze x121 -> x0, local copies, waits for them, and re-layouts: 136 us -> none  [the longest x120 134 us: gru_run(): lax.scan(advance, initial, (drive_all, char_mask), reverse=direction == 1)]
    ppermute x4 -> x30, waiting for transfers between devices: 0.86 us -> 122 us  [the longest x20 119 us: flip(): return lax.ppermute(values, 'dp', [(i, i ^ 1 << bit) for i in range(count)])]
    pallas_call x0 -> x9, Pallas kernels: none -> 92.4 us  [the longest x6 30.9 us: whole_call(): pl.pallas_call(kernel, in_specs=[SMEM] + [VMEM] * (len(args) - 1), out_sp...]
    psum x2 -> x0, blocking collectives: 83.8 us -> none  [the longest x1 45.3 us: per_device(): qkv_shift_out, up_shift_out = lax.psum((merged[1], merged[4]), 'dp')]
    sub x120 -> x0, other arithmetic: 79.4 us -> none  [gate_apply(): return mask_step * moved + (1.0 - mask_step) * carried]
    mul x80 -> x0, other arithmetic: 70.8 us -> none  [the longest x40 45.3 us: gate_apply(): jax.nn.sigmoid(drive_step[:, width:2 * width] + recur_step[:, width:2 * w...]
  transfers between devices with their start and end apart: 12 -> 30, of which waited for: 4 -> 16; matrix products, arithmetic and copies ran while one was open for 68% -> 11% of each run, Pallas kernels for 0% -> 16%
where the time goes in v1:
time: 331 us; the launch traced here: 329 us
  waiting for transfers between devices  122 us (37%)
  Pallas kernels  92.4 us (28%)
  local copies, waits for them, and re-layouts  62 us (19%)
  starting transfers between devices  31 us (9%)
  other arithmetic  18.2 us (5%)
    ppermute x20, waiting for transfers between devices, flip(): return lax.ppermute(values, 'dp', [(i, i ^ 1 << bit) for i in range(count)])  119 us
    unnamed x143, local copies, waits for them, and re-layouts  51.9 us
    pallas_call x6, Pallas kernels, whole_call(): pl.pallas_call(kernel, in_specs=[SMEM] + [VMEM] * (len(args) - 1), out_sp...  30.9 us
    ppermute x20, starting transfers between devices, flip(): return lax.ppermute(values, 'dp', [(i, i ^ 1 << bit) for i in range(count)])  28.4 us
    pallas_call x1, Pallas kernels, gru_bwd(): pl.pallas_call(gru_bwd_kernel, grid=(slots,), in_specs=[full(dc), full(wh...  21.2 us
    pallas_call x1, Pallas kernels, gru_fwd(): pl.pallas_call(gru_fwd_kernel, grid=(slots,), in_specs=[blk(width, fw), b...  20.5 us
    pallas_call x1, Pallas kernels, gru_pack(): pl.pallas_call(lambda *refs: gru_weights(pack, *refs), grid=(count,), in_...  19.9 us
    convert_element_type x18, other arithmetic, added(): return (left.astype(f32) + right.astype(f32)).astype(dtype)  12.1 us
  transfers between devices with their start and end apart: 30, of which 16 were waited for; matrix products, arithmetic and copies ran while one was open for 11% of the time, Pallas kernels for 16%

profile of v1, /device:TPU:0, one launch (start us, length us, event | category | flops | bytes accessed | tf_op | source)
XLA Modules:
  0.0 328.8 jit_solution(4067541270465519157)
XLA Ops:
  2.5 1.5 copy-done.8
  6.7 2.9 attend_fwd.1
  12.9 1.3 collective-permute-done.1.got
  14.3 1.7 copy-done.4
  15.9 3.5 %feed_fwd.1 = (f32[256,768]{1,0:T(8,128)S(1)}, f32[256,1]{1,0:T(8,128)S(1)}, bf16[256,1536]{1,0:T(8,128)(2,1)S(1)}, bf16[256,1536]{1,0:T(8,128)(2,1)S(1)}, f32[2...) custom-call(s32[2]{0:T(128)S(1)} %pad_add_fusion.place.refs_0_, f32[256,768]{1,0:T(8,128)S(1)} %get-tuple-element.62.base, ...), custom_call_target="tpu_custom_call" | custom-call | flops 1048576 | bytes 1024 | tf_op jit(solution)/shard_map/feed_fwd/pallas_call | solution.py:219
  19.9 1.6 fusion.1
  22.5 1.3 copy-done.11
  23.7 20.5 %gru_fwd.1 = (bf16[128,768]{1,0:T(8,128)(2,1)}, bf16[20,128,1536]{2,1,0:T(8,128)(2,1)}, f32[20,128,384]{2,1,0:T(8,128)S(1)}, bf16[20,128,384]{2,1,0:T(8,128)(2,1...) custom-call(bf16[20,128,256]{2,1,0:T(8,128)(2,1)S(1)} %bitcast.159, ...), custom_call_target="tpu_custom_call" | custom-call | flops 1048576 | bytes 1024 | tf_op jit(solution)/shard_map/gru_fwd/pallas_call | solution.py:77
  44.2 1.9 copy-done.13
  46.1 1.9 copy-done.15
  48.0 1.4 copy-done.24
  49.4 1.3 copy-done.25
  51.2 2.2 copy.34
  53.4 1.4 slice.129
  57.1 3.0 copy-done.10
  60.1 9.7 %unite.1 = (bf16[128,768]{1,0:T(8,128)(2,1)}, f32[128,768]{1,0:T(8,128)S(1)}, f32[256,768]{1,0:T(8,128)S(1)}, f32[6,768]{1,0:T(8,128)S(1)}, bf16[768,1152]{1,0:T(8,128)(2,1)}, /*index=5*/bf16[768,1152]{1,0:T(8,128)(2,1)S(1)}) custom-call(s32[2]{0:T(128)S(1)} %pad_add_fusion.place.refs_0_, f32[256,768]{1,0:T(8,128)S(1)} %copy-done.39, ...), custom_call_target="tpu_custom_call" | custom-call | flops 1048576 | bytes 1024 | tf_op jit(solution)/shard_map/unite/pallas_call | solution.py:219
  71.2 2.8 copy-done.16
  75.0 21.2 %gru_bwd.1 = (bf16[20,128,1536]{2,1,0:T(8,128)(2,1)S(1)}, bf16[20,128,1536]{2,1,0:T(8,128)(2,1)}, f32[2,1536]{1,0:T(2,128)S(1)}) custom-call(f32[128,768]{1,0:T(8,128)S(1)} %copy-done.46, bf16[2,1152,384]{2,1,0:T(8,128)(2,1)S(1)} %maximum_bitcast_fusion.wht, bf16[20,128,1536]{2,1,0:T(8,128)(2,1)} %get-tuple-element.85.cof, f32[20,128,384]{2,1,0:T(8,128)S(1)} %copy-done.14, ...), custom_call_target="tpu_custom_call" | custom-call | flops 1048576 | bytes 1024 | tf_op jit(solution)/shard_map/gru_bwd/pallas_call | solution.py:125
  96.2 2.7 collective-permute-start.25
  99.0 4.4 %feed_back.1 = (f32[256,768]{1,0:T(8,128)S(1)}, bf16[256,768]{1,0:T(8,128)(2,1)}, f32[1,1536]{1,0:T(1,128)S(1)}, bf16[384,3072]{1,0:T(8,128)(2,1)}, bf16[384,3072]{1,0:T(8,128)(2,1)S(1)}) custom-call(s32[2]{0:T(128)S(1)} %pad_add_fusion.place.refs_0_, f32[256,768]{1,0:T(8,128)S(1)} %get-tuple-element.68.refs_1_, bf16[256,1536]{1,0:T(8,128)(2,1)S(1)} %copy-done.41, ...), custom_call_target="tpu_custom_call" | custom-call | flops 1048576 | bytes 1024 | tf_op jit(solution)/shard_map/feed_back/pallas_call | solution.py:219
  103.4 1.4 copy-done.22
  105.8 1.3 constant_dynamic-update-slice_fusion
  107.1 1.3 constant_dynamic-update-slice_fusion.7
  108.4 1.3 constant_dynamic-update-slice_fusion.6
  109.7 1.3 constant_dynamic-update-slice_fusion.5
  111.0 1.3 constant_dynamic-update-slice_fusion.4
  112.3 1.3 constant_dynamic-update-slice_fusion.3
  124.0 6.7 %attend_back.1 = (f32[128,768]{1,0:T(8,128)S(1)}, bf16[128,768]{1,0:T(8,128)(2,1)S(1)}, f32[3,768]{1,0:T(4,128)S(1)}, f32[2,384]{1,0:T(2,128)S(1)}, bf16[384,153...) custom-call(s32[2]{0:T(128)S(1)} %pad_add_fusion.place.refs_0_, f32[256,768]{1,0:T(8,128)S(1)} %copy-done.37, ...), custom_call_target="tpu_custom_call" | custom-call | flops 1048576 | bytes 1024 | tf_op jit(solution)/shard_map/attend_back/pallas_call | solution.py:219
  133.1 1.5 collective-permute-start.7
  135.8 1.3 copy-done.12
  137.0 19.9 %gru_pack.1 = (bf16[1088,768]{1,0:T(8,128)(2,1)S(1)}, bf16[1088,768]{1,0:T(8,128)(2,1)}) custom-call(s32[2]{0:T(128)S(1)} %pad_add_fusion.place.refs_0_, bf16[20,128,1536]{2,1,0:T(8,128)(2,1)} %copy-done.6, bf16[20,128,1536]{2,1,0:T(8,128)(2,1)} %get-tuple-element.90.refs_2_, bf16[20,128,384]{2,1,0:T(8,128)(2,1)} %copy-done.24, ...), custom_call_target="tpu_custom_call" | custom-call | flops 1048576 | bytes 1024 | tf_op jit(solution)/shard_map/gru_pack/pallas_call | solution.py:442
  157.5 1.6 collective-permute-start.21
  159.1 1.7 collective-permute-done.6
  160.8 1.8 convert_add_fusion.12
  162.5 1.5 fusion.9
  164.6 1.2 add_convert_fusion.7
  165.8 1.4 fusion.6
  167.2 1.6 collective-permute-start.26
  168.8 1.9 add_convert_fusion
  170.7 1.6 collective-permute-start.12
  172.3 1.4 add_convert_fusion.4
  173.7 6.6 %collective-permute-done.8 = bf16[2,2,48,1536]{3,2,1,0:T(8,128)(2,1)S(1)} collective-permute-done((bf16[2,2,48,1536]{3,2,1,0:T(8,128)(2,1)S(1)}, bf16[2,2,48,1536]{3,2,1,0:T(8,128)(2,1)S(1)}, u32[]{:S(2)}, u32[]{:S(2)}) %collective-permute-start.8) | collective-permute-done | bytes 589856 | tf_op jit(solution)/shard_map/ppermute | solution.py:488
  180.4 1.5 collective-permute-start.9
  181.9 29.9 %collective-permute-done.21 = bf16[384,3072]{1,0:T(8,128)(2,1)} collective-permute-done((bf16[384,3072]{1,0:T(8,128)(2,1)}, bf16[384,3072]{1,0:T(8,128)(2,1)}, u32[]{:S(2)}, u32[]{:S(2)}) %collective-permute-start.21) | collective-permute-done | bytes 2359328 | tf_op jit(solution)/shard_map/ppermute | solution.py:488
  211.8 1.7 fusion.3
  214.5 1.6 collective-permute-start.13
  216.1 1.7 add_convert_fusion.2
  217.8 19.3 %collective-permute-done.9 = bf16[2,48,1536]{2,1,0:T(8,128)(2,1)S(1)} collective-permute-done((bf16[2,48,1536]{2,1,0:T(8,128)(2,1)S(1)}, bf16[2,48,1536]{2,1,0:T(8,128)(2,1)S(1)}, u32[]{:S(2)}, u32[]{:S(2)}) %collective-permute-start.9) | collective-permute-done | bytes 294944 | tf_op jit(solution)/shard_map/ppermute | solution.py:488
  237.1 2.8 collective-permute-start.10
  239.8 5.4 %collective-permute-done.13 = bf16[272,768]{1,0:T(8,128)(2,1)S(1)} collective-permute-done((bf16[272,768]{1,0:T(8,128)(2,1)S(1)}, bf16[272,768]{1,0:T(8,128)(2,1)S(1)}, u32[]{:S(2)}, u32[]{:S(2)}) %collective-permute-start.13) | collective-permute-done | bytes 417824 | tf_op jit(solution)/shard_map/ppermute | solution.py:488
  246.0 5.9 %collective-permute-done.14 = bf16[136,768]{1,0:T(8,128)(2,1)S(1)} collective-permute-done((bf16[136,768]{1,0:T(8,128)(2,1)S(1)}, bf16[136,768]{1,0:T(8,128)(2,1)S(1)}, u32[]{:S(2)}, u32[]{:S(2)}) %collective-permute-start.14) | collective-permute-done | bytes 208928 | tf_op jit(solution)/shard_map/ppermute | solution.py:488
  252.0 2.6 collective-permute-start.15
  255.4 3.3 %collective-permute-done.15 = bf16[136,384]{1,0:T(8,128)(2,1)S(1)} collective-permute-done((bf16[136,384]{1,0:T(8,128)(2,1)S(1)}, bf16[136,384]{1,0:T(8,128)(2,1)S(1)}, u32[]{:S(2)}, u32[]{:S(2)}) %collective-permute-start.15) | collective-permute-done | bytes 104480 | tf_op jit(solution)/shard_map/ppermute | solution.py:488
  258.8 2.8 collective-permute-start.16
  262.2 5.0 %collective-permute-done.16 = bf16[136,384]{1,0:T(8,128)(2,1)S(1)} collective-permute-done((bf16[136,384]{1,0:T(8,128)(2,1)S(1)}, bf16[136,384]{1,0:T(8,128)(2,1)S(1)}, u32[]{:S(2)}, u32[]{:S(2)}) %collective-permute-start.16) | collective-permute-done | bytes 104480 | tf_op jit(solution)/shard_map/ppermute | solution.py:488
  267.2 1.9 collective-permute-start.17
  271.5 3.5 %collective-permute-done.17 = bf16[136,768]{1,0:T(8,128)(2,1)S(1)} collective-permute-done((bf16[136,768]{1,0:T(8,128)(2,1)S(1)}, bf16[136,768]{1,0:T(8,128)(2,1)S(1)}, u32[]{:S(2)}, u32[]{:S(2)}) %collective-permute-start.17) | collective-permute-done | bytes 208928 | tf_op jit(solution)/shard_map/ppermute | solution.py:488
  275.1 1.3 collective-permute-start.18
  276.4 4.3 %collective-permute-done.28 = bf16[96,1152]{1,0:T(8,128)(2,1)S(1)} collective-permute-done((bf16[96,1152]{1,0:T(8,128)(2,1)S(1)}, bf16[96,1152]{1,0:T(8,128)(2,1)S(1)}, u32[]{:S(2)}, u32[]{:S(2)}) %collective-permute-start.28) | collective-permute-done | bytes 221216 | tf_op jit(solution)/shard_map/ppermute | solution.py:488
  281.4 2.9 collective-permute-done.18
  285.2 17.6 %collective-permute-done.19 = bf16[544,768]{1,0:T(8,128)(2,1)S(1)} collective-permute-done((bf16[544,768]{1,0:T(8,128)(2,1)S(1)}, bf16[544,768]{1,0:T(8,128)(2,1)S(1)}, u32[]{:S(2)}, u32[]{:S(2)}) %collective-permute-start.19) | collective-permute-done | bytes 835616 | tf_op jit(solution)/shard_map/ppermute | solution.py:488
  303.7 1.7 collective-permute-start.24
  306.5 13.9 %collective-permute-done.24 = bf16[48,3072]{1,0:T(8,128)(2,1)S(1)} collective-permute-done((bf16[48,3072]{1,0:T(8,128)(2,1)S(1)}, bf16[48,3072]{1,0:T(8,128)(2,1)S(1)}, u32[]{:S(2)}, u32[]{:S(2)}) %collective-permute-start.24) | collective-permute-done | bytes 294944 | tf_op jit(solution)/shard_map/ppermute | solution.py:488
  321.4 3.7 %unpack.1 = (f32[2,256,1152]{2,1,0:T(8,128)}, f32[2,384,1152]{2,1,0:T(8,128)}, f32[512,256]{1,0:T(8,128)}, f32[32,768]{1,0:T(8,128)S(1)}) custom-call(s32[2]{0:T(128)S(1)} %pad_add_fusion.place.refs_0_, bf16[1088,768]{1,0:T(8,128)(2,1)S(1)} %maximum_select_fusion.refs_1_, bf16[1088,768]{1,0:T(8,128)(2,1)S(1)} %collective-permute-done.20.refs_2_), custom_call_target="tpu_custom_call" | custom-call | flops 1048576 | bytes 1024 | tf_op jit(solution)/shard_map/unpack/pallas_call | solution.py:219
  (214 shorter events, 44.3 us)
Async XLA Ops:
  0.6 19.2 %copy-start = (bf16[512,256]{1,0:T(8,128)(2,1)S(1)}, bf16[512,256]{1,0:T(8,128)(2,1)}, u32[]{:S(2)}) copy-start(bf16[512,256]{1,0:T(8,128)(2,1)} %param.31) | copy-start | bytes 786436
  0.7 13.6 %copy-start.2 = (bf16[1,768,1536]{2,1,0:T(8,128)(2,1)S(1)}, bf16[1,768,1536]{2,1,0:T(8,128)(2,1)}, u32[]{:S(2)}) copy-start(bf16[1,768,1536]{2,1,0:T(8,128)(2,1)} %param.25) | copy-start | bytes 7077892
  0.7 1.8 collective-permute-start
  2.5 16.9 %copy-start.32 = (bf16[128,768]{1,0:T(8,128)(2,1)}, bf16[128,768]{1,0:T(8,128)(2,1)S(1)}, u32[]{:S(2)}) copy-start(bf16[128,768]{1,0:T(8,128)(2,1)S(1)} %collective-permute-done.other.refs_11_) | copy-start | bytes 589828
  6.7 7.6 %copy-start.58 = (bf16[1,1536]{1,0:T(2,128)(2,1)S(1)}, bf16[1,1536]{1,0:T(2,128)(2,1)}, u32[]{:S(2)}) copy-start(bf16[1,1536]{1,0:T(2,128)(2,1)} %bup.1) | copy-start | bytes 9220
  12.5 6.9 %copy-start.47 = (bf16[256,384]{1,0:T(8,128)(2,1)}, bf16[256,384]{1,0:T(8,128)(2,1)S(1)}, u32[]{:S(2)}) copy-start(bf16[256,384]{1,0:T(8,128)(2,1)S(1)} %get-tuple-element.75.refs_5_) | copy-start | bytes 589828
  12.6 1.7 collective-permute-start.1
  15.9 3.9 %copy-start.62 = (s32[128,20]{0,1:T(8,128)S(1)}, s32[128,20]{0,1:T(8,128)}, u32[]{:S(2)}) copy-start(s32[128,20]{0,1:T(8,128)} %param.20) | copy-start | bytes 30724
  19.4 2.1 copy-start.17
  19.4 2.2 copy-start.38
  19.4 2.2 copy-start.40
  19.4 2.2 copy-start.42
  19.4 36.8 %collective-permute-start.2 = (bf16[256,768]{1,0:T(8,128)(2,1)}, bf16[256,768]{1,0:T(8,128)(2,1)}, u32[]{:S(2)}, u32[]{:S(2)}) collective-permute-start(bf16[256,768]{1,0:T(8,128)(2,1)} %get-tuple-element.65), channel_id=1, source_target_pairs={{0,1},{1,0},{2,3},{3,2},{4,5},{5,4},{6,7},{7,6},{8,9},{9,8},{10,11... | collective-permute-start | bytes 1179656 | tf_op jit(solution)/shard_map/ppermute | solution.py:483
  19.9 1.7 copy-start.64
  19.9 2.5 copy-start.7
  23.7 27.1 %copy-start.55 = (bf16[128,768]{1,0:T(8,128)(2,1)S(1)}, bf16[128,768]{1,0:T(8,128)(2,1)}, u32[]{:S(2)}) copy-start(bf16[128,768]{1,0:T(8,128)(2,1)} %refs_6_.1) | copy-start | bytes 589828
  44.2 1.9 copy-start.13
  46.1 1.9 copy-start.15
  50.6 5.5 %collective-permute-start.3 = (bf16[128,768]{1,0:T(8,128)(2,1)}, bf16[128,768]{1,0:T(8,128)(2,1)}, u32[]{:S(2)}, u32[]{:S(2)}) collective-permute-start(bf16[128,768]{1,0:T(8,128)(2,1)} %get-tuple-element.66.refs_3_), channel_id=1, source_target_pairs={{0,1},{1,0},{2,3},{3,2},{4,5},{5,4},{6,7},{7,6},{8,9},{9,8},{10,11... | collective-permute-start | bytes 589832 | tf_op jit(solution)/shard_map/ppermute | solution.py:483
  50.8 5.4 %collective-permute-start.4 = (bf16[128,768]{1,0:T(8,128)(2,1)S(1)}, bf16[128,768]{1,0:T(8,128)(2,1)}, u32[]{:S(2)}, u32[]{:S(2)}) collective-permute-start(bf16[128,768]{1,0:T(8,128)(2,1)S(1)} %copy-done.55), channel_id=1, source_target_pairs={{0,1},{1,0},{2,3},{3,2},{4,5},{5,4},{6,7},{7,6},{8,9},{9,8},{10,11... | collective-permute-start | bytes 589832 | tf_op jit(solution)/shard_map/ppermute | solution.py:483
  53.4 2.6 copy-start.63
  57.1 3.0 copy-start.10
  60.1 11.1 %copy-start.14 = (f32[20,128,384]{2,1,0:T(8,128)S(1)}, f32[20,128,384]{2,1,0:T(8,128)}, u32[]{:S(2)}) copy-start(f32[20,128,384]{2,1,0:T(8,128)} %copy-done.13) | copy-start | bytes 11796484
  71.2 24.9 %copy-start.26 = (bf16[768,1152]{1,0:T(8,128)(2,1)}, bf16[768,1152]{1,0:T(8,128)(2,1)S(1)}, u32[]{:S(2)}) copy-start(bf16[768,1152]{1,0:T(8,128)(2,1)S(1)} %get-tuple-element.106) | copy-start | bytes 5308420
  71.2 2.8 copy-start.16
  75.0 24.0 %copy-start.3 = (bf16[1,768,1536]{2,1,0:T(8,128)(2,1)S(1)}, bf16[1,768,1536]{2,1,0:T(8,128)(2,1)}, u32[]{:S(2)}) copy-start(bf16[1,768,1536]{2,1,0:T(8,128)(2,1)} %param.25) | copy-start | bytes 7077892
  75.0 24.0 %copy-start.5 = (bf16[1,1536,768]{2,1,0:T(8,128)(2,1)S(1)}, bf16[1,1536,768]{2,1,0:T(8,128)(2,1)}, u32[]{:S(2)}) copy-start(bf16[1,1536,768]{2,1,0:T(8,128)(2,1)} %param.27) | copy-start | bytes 7077892
  75.0 24.0 %copy-start.18 = (f32[256,768]{1,0:T(8,128)S(1)}, f32[256,768]{1,0:T(8,128)}, u32[]{:S(2)}) copy-start(f32[256,768]{1,0:T(8,128)} %copy-done.17) | copy-start | bytes 2359300
  75.0 24.0 %copy-start.41 = (bf16[256,1536]{1,0:T(8,128)(2,1)S(1)}, bf16[256,1536]{1,0:T(8,128)(2,1)}, u32[]{:S(2)}) copy-start(bf16[256,1536]{1,0:T(8,128)(2,1)} %copy-done.40) | copy-start | bytes 2359300
  75.0 24.0 %copy-start.43 = (bf16[256,1536]{1,0:T(8,128)(2,1)S(1)}, bf16[256,1536]{1,0:T(8,128)(2,1)}, u32[]{:S(2)}) copy-start(bf16[256,1536]{1,0:T(8,128)(2,1)} %copy-done.42) | copy-start | bytes 2359300
  96.2 7.3 %copy-start.6 = (bf16[20,128,1536]{2,1,0:T(8,128)(2,1)}, bf16[20,128,1536]{2,1,0:T(8,128)(2,1)S(1)}, u32[]{:S(2)}) copy-start(bf16[20,128,1536]{2,1,0:T(8,128)(2,1)S(1)} %get-tuple-element.89.refs_1_) | copy-start | bytes 23592964
  96.2 69.5 %collective-permute-start.25 = (bf16[768,1152]{1,0:T(8,128)(2,1)}, bf16[768,1152]{1,0:T(8,128)(2,1)}, u32[]{:S(2)}, u32[]{:S(2)}) collective-permute-start(bf16[768,1152]{1,0:T(8,128)(2,1)} %get-tuple-element.107), channel_id=1, source_target_pairs={{0,2},{2,0},{4,6},{6,4},{8,10},{10,8},{12,14},{14,12},{16,18},{18,... | collective-permute-start | bytes 5308424 | tf_op jit(solution)/shard_map/ppermute | solution.py:488
  99.0 15.3 %copy-start.57 = (f32[6,768]{1,0:T(8,128)S(1)}, f32[6,768]{1,0:T(8,128)}, u32[]{:S(2)}) copy-start(f32[6,768]{1,0:T(8,128)} %copy-done.56) | copy-start | bytes 55300
  99.0 15.9 %copy-start.9 = (bf16[1,768,3,384]{3,1,2,0:T(8,128)(2,1)S(1)}, bf16[1,768,3,384]{3,1,2,0:T(8,128)(2,1)}, u32[]{:S(2)}) copy-start(bf16[1,768,3,384]{3,1,2,0:T(8,128)(2,1)} %param.22) | copy-start | bytes 5308420
  99.0 15.9 %copy-start.31 = (bf16[128,768]{1,0:T(8,128)(2,1)S(1)}, bf16[128,768]{1,0:T(8,128)(2,1)}, u32[]{:S(2)}) copy-start(bf16[128,768]{1,0:T(8,128)(2,1)} %refs_10_.1) | copy-start | bytes 589828
  105.7 9.2 %collective-permute-start.5 = (bf16[256,768]{1,0:T(8,128)(2,1)}, bf16[256,768]{1,0:T(8,128)(2,1)}, u32[]{:S(2)}, u32[]{:S(2)}) collective-permute-start(bf16[256,768]{1,0:T(8,128)(2,1)} %get-tuple-element.73), channel_id=1, source_target_pairs={{0,1},{1,0},{2,3},{3,2},{4,5},{5,4},{6,7},{7,6},{8,9},{9,8},{10,11... | collective-permute-start | bytes 1179656 | tf_op jit(solution)/shard_map/ppermute | solution.py:483
  133.1 29.4 %collective-permute-start.7 = (bf16[384,1536]{1,0:T(8,128)(2,1)}, bf16[384,1536]{1,0:T(8,128)(2,1)}, u32[]{:S(2)}, u32[]{:S(2)}) collective-permute-start(bf16[384,1536]{1,0:T(8,128)(2,1)} %get-tuple-element.83), channel_id=1, source_target_pairs={{0,8},{2,10},{4,12},{6,14},{8,0},{10,2},{12,4},{14,6},{16,24},{18,... | collective-permute-start | bytes 3538952 | tf_op jit(solution)/shard_map/ppermute | solution.py:488
  137.0 20.1 %copy-start.61 = (bf16[128,768]{1,0:T(8,128)(2,1)S(1)}, bf16[128,768]{1,0:T(8,128)(2,1)}, u32[]{:S(2)}) copy-start(bf16[128,768]{1,0:T(8,128)(2,1)} %copy-done.60) | copy-start | bytes 589828
  156.9 7.6 %copy-start.29 = (bf16[384,1536]{1,0:T(8,128)(2,1)S(1)}, bf16[384,1536]{1,0:T(8,128)(2,1)}, u32[]{:S(2)}) copy-start(bf16[384,1536]{1,0:T(8,128)(2,1)} %copy-done.28) | copy-start | bytes 3538948
  156.9 11.9 %collective-permute-start.11 = (bf16[1088,768]{1,0:T(8,128)(2,1)}, bf16[1088,768]{1,0:T(8,128)(2,1)}, u32[]{:S(2)}, u32[]{:S(2)}) collective-permute-start(bf16[1088,768]{1,0:T(8,128)(2,1)} %get-tuple-element.99), channel_id=1, source_target_pairs={{0,1},{1,0},{2,3},{3,2},{4,5},{5,4},{6,7},{7,6},{8,9},{9,8},{10,11... | collective-permute-start | bytes 5013512 | tf_op jit(solution)/shard_map/ppermute | solution.py:483
  157.2 3.6 %collective-permute-start.6 = (bf16[128,768]{1,0:T(8,128)(2,1)S(1)}, bf16[128,768]{1,0:T(8,128)(2,1)S(1)}, u32[]{:S(2)}, u32[]{:S(2)}) collective-permute-start(bf16[128,768]{1,0:T(8,128)(2,1)S(1)} %copy-done.61), channel_id=1, source_target_pairs={{0,1},{1,0},{2,3},{3,2},{4,5},{5,4},{6,7},{7,6},{8,9},{9,8},{10,11... | collective-permute-start | bytes 589832 | tf_op jit(solution)/shard_map/ppermute | solution.py:483
  157.5 54.4 %collective-permute-start.21 = (bf16[384,3072]{1,0:T(8,128)(2,1)}, bf16[384,3072]{1,0:T(8,128)(2,1)}, u32[]{:S(2)}, u32[]{:S(2)}) collective-permute-start(bf16[384,3072]{1,0:T(8,128)(2,1)} %get-tuple-element.102), channel_id=1, source_target_pairs={{0,4},{2,6},{4,0},{6,2},{8,12},{10,14},{12,8},{14,10},{16,20},{18,... | collective-permute-start | bytes 7077896 | tf_op jit(solution)/shard_map/ppermute | solution.py:488
  162.5 3.2 copy-start.27
  164.1 16.2 %collective-permute-start.8 = (bf16[2,2,48,1536]{3,2,1,0:T(8,128)(2,1)S(1)}, bf16[2,2,48,1536]{3,2,1,0:T(8,128)(2,1)S(1)}, u32[]{:S(2)}, u32[]{:S(2)}) collective-permute-start(bf16[2,2,48,1536]{3,2,1,0:T(8,128)(2,1)S(1)} %fusion.9), channel_id=1, source_target_pairs={{0,2},{2,0},{4,6},{6,4},{8,10},{10,8},{12,14},{14,12},{16,18},{18,... | collective-permute-start | bytes 1769480 | tf_op jit(solution)/shard_map/ppermute | solution.py:488
  167.2 87.5 %collective-permute-start.26 = (bf16[2,2,96,1152]{3,2,1,0:T(8,128)(2,1)S(1)}, bf16[2,2,96,1152]{3,2,1,0:T(8,128)(2,1)S(1)}, u32[]{:S(2)}, u32[]{:S(2)}) collective-permute-start(bf16[2,2,96,1152]{3,2,1,0:T(8,128)(2,1)S(1)} %fusion.6), channel_id=1, source_target_pairs={{0,4},{2,6},{4,0},{6,2},{8,12},{10,14},{12,8},{14,10},{16,20},{18,... | collective-permute-start | bytes 2654216 | tf_op jit(solution)/shard_map/ppermute | solution.py:488
  170.7 41.1 %copy-start.23 = (bf16[384,3072]{1,0:T(8,128)(2,1)S(1)}, bf16[384,3072]{1,0:T(8,128)(2,1)}, u32[]{:S(2)}) copy-start(bf16[384,3072]{1,0:T(8,128)(2,1)} %copy-done.22) | copy-start | bytes 7077892
  170.7 43.5 %collective-permute-start.12 = (bf16[544,768]{1,0:T(8,128)(2,1)S(1)}, bf16[544,768]{1,0:T(8,128)(2,1)S(1)}, u32[]{:S(2)}, u32[]{:S(2)}) collective-permute-start(bf16[544,768]{1,0:T(8,128)(2,1)S(1)} %constant_dynamic-slice_fusion.7), channel_id=1, source_target_pairs={{0,2},{2,0},{4,6},{6,4},{8,10},{10,8},{12,14},{14,12},{16,18},{18,... | collective-permute-start | bytes 2506760 | tf_op jit(solution)/shard_map/ppermute | solution.py:488
  180.4 56.6 %collective-permute-start.9 = (bf16[2,48,1536]{2,1,0:T(8,128)(2,1)S(1)}, bf16[2,48,1536]{2,1,0:T(8,128)(2,1)S(1)}, u32[]{:S(2)}, u32[]{:S(2)}) collective-permute-start(bf16[2,48,1536]{2,1,0:T(8,128)(2,1)S(1)} %get-tuple-element.137), channel_id=1, source_target_pairs={{0,4},{2,6},{4,0},{6,2},{8,12},{10,14},{12,8},{14,10},{16,20},{18,... | collective-permute-start | bytes 884744 | tf_op jit(solution)/shard_map/ppermute | solution.py:488
  213.5 67.4 %collective-permute-start.22 = (bf16[2,2,48,3072]{3,2,1,0:T(8,128)(2,1)S(1)}, bf16[2,2,48,3072]{3,2,1,0:T(8,128)(2,1)S(1)}, u32[]{:S(2)}, u32[]{:S(2)}) collective-permute-start(bf16[2,2,48,3072]{3,2,1,0:T(8,128)(2,1)S(1)} %fusion.3), channel_id=1, source_target_pairs={{0,2},{2,0},{4,6},{6,4},{8,10},{10,8},{12,14},{14,12},{16,18},{18,... | collective-permute-start | bytes 3538952 | tf_op jit(solution)/shard_map/ppermute | solution.py:488
  214.5 30.8 %collective-permute-start.13 = (bf16[272,768]{1,0:T(8,128)(2,1)S(1)}, bf16[272,768]{1,0:T(8,128)(2,1)S(1)}, u32[]{:S(2)}, u32[]{:S(2)}) collective-permute-start(bf16[272,768]{1,0:T(8,128)(2,1)S(1)} %constant_dynamic-slice_fusion.6), channel_id=1, source_target_pairs={{0,4},{2,6},{4,0},{6,2},{8,12},{10,14},{12,8},{14,10},{16,20},{18,... | collective-permute-start | bytes 1253384 | tf_op jit(solution)/shard_map/ppermute | solution.py:488
  237.1 8.9 %collective-permute-start.10 = (bf16[48,1536]{1,0:T(8,128)(2,1)S(1)}, bf16[48,1536]{1,0:T(8,128)(2,1)S(1)}, u32[]{:S(2)}, u32[]{:S(2)}) collective-permute-start(bf16[48,1536]{1,0:T(8,128)(2,1)S(1)} %fusion.27), channel_id=1, source_target_pairs={{0,16},{2,18},{4,20},{6,22},{8,24},{10,26},{12,28},{14,30},{16,0},... | collective-permute-start | bytes 442376 | tf_op jit(solution)/shard_map/ppermute | solution.py:488
  245.4 6.5 %collective-permute-start.14 = (bf16[136,768]{1,0:T(8,128)(2,1)S(1)}, bf16[136,768]{1,0:T(8,128)(2,1)S(1)}, u32[]{:S(2)}, u32[]{:S(2)}) collective-permute-start(bf16[136,768]{1,0:T(8,128)(2,1)S(1)} %constant_dynamic-slice_fusion.5), channel_id=1, source_target_pairs={{0,8},{2,10},{4,12},{6,14},{8,0},{10,2},{12,4},{14,6},{16,24},{18,... | collective-permute-start | bytes 626696 | tf_op jit(solution)/shard_map/ppermute | solution.py:488
  252.0 6.7 %collective-permute-start.15 = (bf16[136,384]{1,0:T(8,128)(2,1)S(1)}, bf16[136,384]{1,0:T(8,128)(2,1)S(1)}, u32[]{:S(2)}, u32[]{:S(2)}) collective-permute-start(bf16[136,384]{1,0:T(8,128)(2,1)S(1)} %constant_dynamic-slice_fusion.4), channel_id=1, source_target_pairs={{0,16},{2,18},{4,20},{6,22},{8,24},{10,26},{12,28},{14,30},{16,0},... | collective-permute-start | bytes 313352 | tf_op jit(solution)/shard_map/ppermute | solution.py:488
  254.9 15.2 %collective-permute-start.27 = (bf16[2,96,1152]{2,1,0:T(8,128)(2,1)S(1)}, bf16[2,96,1152]{2,1,0:T(8,128)(2,1)S(1)}, u32[]{:S(2)}, u32[]{:S(2)}) collective-permute-start(bf16[2,96,1152]{2,1,0:T(8,128)(2,1)S(1)} %get-tuple-element.135), channel_id=1, source_target_pairs={{0,8},{2,10},{4,12},{6,14},{8,0},{10,2},{12,4},{14,6},{16,24},{18,... | collective-permute-start | bytes 1327112 | tf_op jit(solution)/shard_map/ppermute | solution.py:488
  258.8 8.4 %collective-permute-start.16 = (bf16[136,384]{1,0:T(8,128)(2,1)S(1)}, bf16[136,384]{1,0:T(8,128)(2,1)S(1)}, u32[]{:S(2)}, u32[]{:S(2)}) collective-permute-start(bf16[136,384]{1,0:T(8,128)(2,1)S(1)} %add_convert_fusion.10), channel_id=1, source_target_pairs={{0,16},{2,18},{4,20},{6,22},{8,24},{10,26},{12,28},{14,30},{16,0},... | collective-permute-start | bytes 313352 | tf_op jit(solution)/shard_map/ppermute | solution.py:488
  267.2 7.8 %collective-permute-start.17 = (bf16[136,768]{1,0:T(8,128)(2,1)S(1)}, bf16[136,768]{1,0:T(8,128)(2,1)S(1)}, u32[]{:S(2)}, u32[]{:S(2)}) collective-permute-start(bf16[136,768]{1,0:T(8,128)(2,1)S(1)} %maximum_select_fusion.3), channel_id=1, source_target_pairs={{0,8},{2,10},{4,12},{6,14},{8,0},{10,2},{12,4},{14,6},{16,24},{18,... | collective-permute-start | bytes 626696 | tf_op jit(solution)/shard_map/ppermute | solution.py:488
  270.2 10.6 %collective-permute-start.28 = (bf16[96,1152]{1,0:T(8,128)(2,1)S(1)}, bf16[96,1152]{1,0:T(8,128)(2,1)S(1)}, u32[]{:S(2)}, u32[]{:S(2)}) collective-permute-start(bf16[96,1152]{1,0:T(8,128)(2,1)S(1)} %fusion.25), channel_id=1, source_target_pairs={{0,16},{2,18},{4,20},{6,22},{8,24},{10,26},{12,28},{14,30},{16,0},... | collective-permute-start | bytes 663560 | tf_op jit(solution)/shard_map/ppermute | solution.py:488
  275.1 9.2 %collective-permute-start.18 = (bf16[272,768]{1,0:T(8,128)(2,1)S(1)}, bf16[272,768]{1,0:T(8,128)(2,1)S(1)}, u32[]{:S(2)}, u32[]{:S(2)}) collective-permute-start(bf16[272,768]{1,0:T(8,128)(2,1)S(1)} %maximum_select_fusion.2), channel_id=1, source_target_pairs={{0,4},{2,6},{4,0},{6,2},{8,12},{10,14},{12,8},{14,10},{16,20},{18,... | collective-permute-start | bytes 1253384 | tf_op jit(solution)/shard_map/ppermute | solution.py:488
  280.9 4.2 %collective-permute-start.29 = (bf16[96,1152]{1,0:T(8,128)(2,1)S(1)}, bf16[96,1152]{1,0:T(8,128)(2,1)S(1)}, u32[]{:S(2)}, u32[]{:S(2)}) collective-permute-start(bf16[96,1152]{1,0:T(8,128)(2,1)S(1)} %fusion.17), channel_id=1, source_target_pairs={{0,1},{1,0},{2,3},{3,2},{4,5},{5,4},{6,7},{7,6},{8,9},{9,8},{10,11... | collective-permute-start | bytes 663560 | tf_op jit(solution)/shard_map/ppermute | solution.py:483
  281.4 22.3 %collective-permute-start.23 = (bf16[2,48,3072]{2,1,0:T(8,128)(2,1)S(1)}, bf16[2,48,3072]{2,1,0:T(8,128)(2,1)S(1)}, u32[]{:S(2)}, u32[]{:S(2)}) collective-permute-start(bf16[2,48,3072]{2,1,0:T(8,128)(2,1)S(1)} %get-tuple-element.133), channel_id=1, source_target_pairs={{0,8},{2,10},{4,12},{6,14},{8,0},{10,2},{12,4},{14,6},{16,24},{18,... | collective-permute-start | bytes 1769480 | tf_op jit(solution)/shard_map/ppermute | solution.py:488
  284.7 18.1 %collective-permute-start.19 = (bf16[544,768]{1,0:T(8,128)(2,1)S(1)}, bf16[544,768]{1,0:T(8,128)(2,1)S(1)}, u32[]{:S(2)}, u32[]{:S(2)}) collective-permute-start(bf16[544,768]{1,0:T(8,128)(2,1)S(1)} %maximum_select_fusion.1), channel_id=1, source_target_pairs={{0,2},{2,0},{4,6},{6,4},{8,10},{10,8},{12,14},{14,12},{16,18},{18,... | collective-permute-start | bytes 2506760 | tf_op jit(solution)/shard_map/ppermute | solution.py:488
  303.6 17.8 %collective-permute-start.20 = (bf16[1088,768]{1,0:T(8,128)(2,1)S(1)}, bf16[1088,768]{1,0:T(8,128)(2,1)S(1)}, u32[]{:S(2)}, u32[]{:S(2)}) collective-permute-start(bf16[1088,768]{1,0:T(8,128)(2,1)S(1)} %maximum_select_fusion.refs_1_), channel_id=1, source_target_pairs={{0,1},{1,0},{2,3},{3,2},{4,5},{5,4},{6,7},{7,6},{8,9},{9,8},{10,11... | collective-permute-start | bytes 5013512 | tf_op jit(solution)/shard_map/ppermute | solution.py:483
  303.7 16.7 %collective-permute-start.24 = (bf16[48,3072]{1,0:T(8,128)(2,1)S(1)}, bf16[48,3072]{1,0:T(8,128)(2,1)S(1)}, u32[]{:S(2)}, u32[]{:S(2)}) collective-permute-start(bf16[48,3072]{1,0:T(8,128)(2,1)S(1)} %fusion.21), channel_id=1, source_target_pairs={{0,16},{2,18},{4,20},{6,22},{8,24},{10,26},{12,28},{14,30},{16,0},... | collective-permute-start | bytes 884744 | tf_op jit(solution)/shard_map/ppermute | solution.py:488
  320.5 8.3 %copy-start.1 = (bf16[512,256]{1,0:T(8,128)(2,1)S(1)}, bf16[512,256]{1,0:T(8,128)(2,1)}, u32[]{:S(2)}) copy-start(bf16[512,256]{1,0:T(8,128)(2,1)} %param.31) | copy-start | bytes 786436
  (31 other events, 31.3 us)
